TPU v7x, 256 devices: a whole 4x4x8 slice. The times are simulated.
256 devices in a mesh: gx: 16 (over y_hi, x, core), gy: 16 (over y_lo, z).
Axes of the slice: x: 4, y: 4 (y_hi: 2, y_lo: 2; y = y_hi * 2 + y_lo), z: 8, core: 2. Of those that a mesh axis runs over, the one named last changes fastest.
Arguments:
- subspace: bfloat16 [16, 16, 2048, 256], P('gx', 'gy'), may hold values from -200 to 200
- hamiltonian: bfloat16 [16, 16, 32, 64, 512], P('gx', 'gy'), may hold values from -0.125 to 0.125
- neighbours: int32 [16, 16, 32, 8], P('gx', 'gy'), may hold values from 0 to 39
- send_lists: int32 [16, 16, 4, 2], P('gx', 'gy'), may hold values from 0 to 31
- rotation: bfloat16 [256, 256], replicated, may hold values from -0.375 to 0.375
Outputs:
- rotated: bfloat16 [16, 16, 2048, 256], P('gx', 'gy')
- margin: float32 [256, 256], P(('gx', 'gy'))
Inputs may be any that keep to these rules, and one draw needn't show every extreme that they name: `neighbours`: slots below 32 are the device's own blocks; slot 32 + d * 2 + h is the h-th block of packet d received.
All inputs are finite; a program needn't handle non-finite values.
Results may differ from a plain program's by a relative error of at most 0.013.
Values may be sent and summed in bfloat16 or wider, within the bound.
No kernel may reach another device: no remote copies, remote signals or barrier semaphores. Data moves between devices by JAX's collectives and lax.ppermute only.
A program may use at most 64 MiB of HBM per device.

v0:
```python
import jax
import jax.numpy as jnp
from jax import lax
from jax.sharding import PartitionSpec as P

STEPS = 6


center_shift = 0.1
half_width = 0.8


def from_behind(value, axis, steps):
    count = lax.axis_size(axis)
    leading, last = (max(0, -steps), min(count, count - steps))
    return lax.ppermute(value, axis, [(source, source + steps) for source in range(leading, last)])


def scaled_apply(state, couplings, columns_of, outgoing):
    blocks, orbitals, columns = state.shape
    halo_count = outgoing.shape[1]
    lowered = state.astype(jnp.bfloat16)
    packets = lowered[outgoing.reshape(-1)].reshape(4, halo_count, orbitals, columns)
    received = []
    for offset, slot in ((1, 0), (-1, 1)):
        received.append(from_behind(packets[slot], "gx", offset))
    for offset, slot in ((1, 2), (-1, 3)):
        received.append(from_behind(packets[slot], "gy", offset))
    extended = jnp.concatenate([lowered] + received, axis=0)
    gathered = extended[columns_of].reshape(blocks, -1, columns)
    product = jnp.einsum("rak,rkc->rac", couplings, gathered, preferred_element_type=jnp.float32)
    return (product - center_shift * state) / half_width


def on_device(subspace, hamiltonian, neighbours, send_lists, rotation):
    couplings = hamiltonian[0, 0]
    columns_of = neighbours[0, 0]
    outgoing = send_lists[0, 0]
    blocks = couplings.shape[0]
    orbitals = couplings.shape[1]
    columns = subspace.shape[3]
    start_state = subspace[0, 0].astype(jnp.float32).reshape(blocks, orbitals, columns)
    previous = start_state
    present = scaled_apply(start_state, couplings, columns_of, outgoing)
    for degree in range(STEPS - 1):
        following = 2.0 * scaled_apply(present, couplings, columns_of, outgoing) - previous
        previous, present = (present, following)
    filtered = present.astype(jnp.bfloat16).reshape(blocks * orbitals, columns)
    rotated_full = jnp.dot(filtered, rotation, preferred_element_type=jnp.float32)
    rotated = rotated_full.astype(jnp.bfloat16).reshape(subspace.shape)
    devices_all = lax.axis_size("gx") * lax.axis_size("gy")
    orbital_total = blocks * orbitals * devices_all
    own_rows = columns // devices_all
    local_gram = lax.dot_general(
        filtered, filtered, (((0,), (0,)), ((), ())), preferred_element_type=jnp.float32
    )
    gram = lax.psum(local_gram, ("gx", "gy"))
    rotation_wide = rotation.astype(jnp.float32)
    position = lax.axis_index(("gx", "gy"))
    chosen = lax.dynamic_slice_in_dim(rotation_wide, position * own_rows, own_rows, 1)
    right_side = jnp.dot(gram, rotation_wide, precision=lax.Precision.HIGHEST)
    margin = lax.dot_general(
        chosen, right_side, (((0,), (0,)), ((), ())), precision=lax.Precision.HIGHEST
    )
    return (rotated, margin / orbital_total)


def solution(mesh):
    return jax.shard_map(
        on_device,
        mesh=mesh,
        in_specs=(
            P("gx", "gy", None, None),
            P("gx", "gy", None, None, None),
            P("gx", "gy", None, None),
            P("gx", "gy", None, None),
            P(),
        ),
        out_specs=(P("gx", "gy", None, None), P(("gx", "gy"), None)),
        check_vma=False,
    )
```

profile of v0, /device:TPU:1, one launch (start us, length us, event | category | flops | bytes accessed | tf_op | source)
XLA Modules:
  0.0 503.6 jit_solution(15919677934829795639)
XLA Ops:
  10.7 4.5 collective-permute-start
  27.8 8.7 %gather_fusion.1 = bf16[256,64,256]{2,1,0:T(8,128)(2,1)} fusion(bf16[40,64,256]{2,1,0:T(8,128)(2,1)S(1)} %constant_dynamic-update-slice_fusion, s32[1024]{0:T(1024)S(1)} %pad_clamp_fusion), kind=kCustom, calls=%fused_computation.1 | custom fusion | bytes 16778240 | tf_op jit(solution)/shard_map/gather | solution.py:30
  36.4 6.8 %constant_dynamic-update-slice_fusion.9 = (bf16[40,64,256]{2,1,0:T(8,128)(2,1)S(1)}, bf16[32,64,256]{2,1,0:T(8,128)(2,1)}, f32[32,64,256]{2,1,0:T(8,128)}) fusion(bf16[32,64,256]{2,1,0:T(8,128)(2,1)} %bitcast.111, bf16[32,512,256]{2,1,0:T(8,128)(2,1)} %bitcast.103, bf16[1,1,32,64,512]{4,3,2,1,0:T(8,128)(2,1)S(1)} %copy-done), kind=kOutput, calls=%fused_computation.56 | convolution fusion | flops 539492352 | bytes 15728640 | tf_op jit(solution)/shard_map/rak,rkc->rac/dot_general | solution.py:31
  46.6 3.9 collective-permute-start.4
  52.5 4.3 collective-permute-start.6
  61.9 8.7 %gather_fusion.3 = bf16[256,64,256]{2,1,0:T(8,128)(2,1)} fusion(bf16[40,64,256]{2,1,0:T(8,128)(2,1)S(1)} %constant_dynamic-update-slice_fusion.5, s32[1024]{0:T(1024)S(1)} %pad_clamp_fusion), kind=kCustom, calls=%fused_computation.3 | custom fusion | bytes 16778240 | tf_op jit(solution)/shard_map/gather | solution.py:30
  70.6 7.5 %constant_dynamic-update-slice_fusion.14 = (bf16[40,64,256]{2,1,0:T(8,128)(2,1)S(1)}, bf16[32,64,256]{2,1,0:T(8,128)(2,1)}, f32[32,64,256]{2,1,0:T(8,128)}) fusion(bf16[32,64,256]{2,1,0:T(8,128)(2,1)} %bitcast.112, f32[32,64,256]{2,1,0:T(8,128)} %get-tuple-element.36, bf16[32,512,256]{2,1,0:T(8,128)(2,1)} %bitcast.107, ...), kind=kOutput, calls=%fused_computation.61 | convolution fusion | flops 540016640 | bytes 17825792 | tf_op jit(solution)/shard_map/rak,rkc->rac/dot_general | solution.py:31
  81.5 4.9 collective-permute-start.8
  88.3 4.6 collective-permute-start.10
  94.5 4.9 collective-permute-done.11
  99.4 8.7 %gather_fusion.5 = bf16[256,64,256]{2,1,0:T(8,128)(2,1)} fusion(bf16[40,64,256]{2,1,0:T(8,128)(2,1)S(1)} %constant_dynamic-update-slice_fusion.10, s32[1024]{0:T(1024)S(1)} %pad_clamp_fusion), kind=kCustom, calls=%fused_computation.5 | custom fusion | bytes 16778240 | tf_op jit(solution)/shard_map/gather | solution.py:30
  108.1 7.8 %constant_dynamic-update-slice_fusion.19 = (bf16[40,64,256]{2,1,0:T(8,128)(2,1)S(1)}, bf16[32,64,256]{2,1,0:T(8,128)(2,1)}, f32[32,64,256]{2,1,0:T(8,128)}) fusion(f32[32,64,256]{2,1,0:T(8,128)} %get-tuple-element.36, f32[32,64,256]{2,1,0:T(8,128)} %get-tuple-element.37, bf16[32,512,256]{2,1,0:T(8,128)(2,1)} %bitcast.104, ...), kind=kOutput, calls=%fused_computation.66 | convolution fusion | flops 540016640 | bytes 18874368 | tf_op jit(solution)/shard_map/rak,rkc->rac/dot_general | solution.py:31
  119.3 4.8 collective-permute-start.12
  126.1 4.9 collective-permute-start.14
  132.3 3.9 collective-permute-done.15
  136.2 8.7 %gather_fusion.7 = bf16[256,64,256]{2,1,0:T(8,128)(2,1)} fusion(bf16[40,64,256]{2,1,0:T(8,128)(2,1)S(1)} %constant_dynamic-update-slice_fusion.15, s32[1024]{0:T(1024)S(1)} %pad_clamp_fusion), kind=kCustom, calls=%fused_computation.7 | custom fusion | bytes 16778240 | tf_op jit(solution)/shard_map/gather | solution.py:30
  144.9 7.8 %constant_dynamic-update-slice_fusion.24 = (bf16[40,64,256]{2,1,0:T(8,128)(2,1)S(1)}, bf16[32,64,256]{2,1,0:T(8,128)(2,1)}, f32[32,64,256]{2,1,0:T(8,128)}) fusion(f32[32,64,256]{2,1,0:T(8,128)} %get-tuple-element.37, f32[32,64,256]{2,1,0:T(8,128)} %get-tuple-element.38, bf16[32,512,256]{2,1,0:T(8,128)(2,1)} %bitcast.105, ...), kind=kOutput, calls=%fused_computation.71 | convolution fusion | flops 539492352 | bytes 18874368 | tf_op jit(solution)/shard_map/rak,rkc->rac/dot_general | solution.py:31
  156.1 4.8 collective-permute-start.16
  171.5 8.7 %gather_fusion.9 = bf16[256,64,256]{2,1,0:T(8,128)(2,1)} fusion(bf16[40,64,256]{2,1,0:T(8,128)(2,1)S(1)} %constant_dynamic-update-slice_fusion.20, s32[1024]{0:T(1024)S(1)} %pad_clamp_fusion), kind=kCustom, calls=%fused_computation.9 | custom fusion | bytes 16778240 | tf_op jit(solution)/shard_map/gather | solution.py:30
  180.2 7.8 %constant_dynamic-update-slice_fusion.29 = (bf16[40,64,256]{2,1,0:T(8,128)(2,1)S(1)}, bf16[32,64,256]{2,1,0:T(8,128)(2,1)}, f32[32,64,256]{2,1,0:T(8,128)}) fusion(f32[32,64,256]{2,1,0:T(8,128)} %get-tuple-element.38, f32[32,64,256]{2,1,0:T(8,128)} %get-tuple-element.39, bf16[32,512,256]{2,1,0:T(8,128)(2,1)} %bitcast.106, ...), kind=kOutput, calls=%fused_computation.76 | convolution fusion | flops 539492352 | bytes 18874368 | tf_op jit(solution)/shard_map/rak,rkc->rac/dot_general | solution.py:31
  192.1 5.1 %collective-permute-start.20 = (bf16[2,64,256]{2,1,0:T(8,128)(2,1)}, bf16[2,64,256]{2,1,0:T(8,128)(2,1)}, u32[]{:S(2)}, u32[]{:S(2)}) collective-permute-start(bf16[2,64,256]{2,1,0:T(8,128)(2,1)} %get-tuple-element.15), channel_id=1, source_target_pairs={{0,16},{16,32},{32,48},{48,64},{64,80},{80,96},{96,112},{112,128},... | collective-permute-start | bytes 196616 | tf_op jit(solution)/shard_map/ppermute | solution.py:16
  207.4 8.7 %gather_fusion.11 = bf16[256,64,256]{2,1,0:T(8,128)(2,1)} fusion(bf16[40,64,256]{2,1,0:T(8,128)(2,1)S(1)} %constant_dynamic-update-slice_fusion.25, s32[1024]{0:T(1024)S(1)} %pad_clamp_fusion), kind=kCustom, calls=%fused_computation.11 | custom fusion | bytes 16778240 | tf_op jit(solution)/shard_map/gather | solution.py:30
  216.1 6.1 %fusion.4 = bf16[32,64,256]{2,1,0:T(8,128)(2,1)S(1)} fusion(f32[32,64,256]{2,1,0:T(8,128)} %get-tuple-element.39, f32[32,64,256]{2,1,0:T(8,128)} %get-tuple-element.40, bf16[32,512,256]{2,1,0:T(8,128)(2,1)} %bitcast.108, bf16[1,1,32,64,512]{4,3,2,1,0:T(8,128)(2,1)S(1)} %copy-done), kind=kOutput, calls=%fused_computation.20 | convolution fusion | flops 539492352 | bytes 15728640 | tf_op jit(solution)/shard_map/rak,rkc->rac/dot_general | solution.py:31
  224.8 270.0 %all-reduce.2.cloned.1.call-done = f32[256,256]{1,0:T(8,128)} async-done(((f32[256,256]{1,0:T(8,128)}), f32[256,256]{1,0:T(8,128)}) %all-reduce.2.cloned.1.call-update) | async-done | bytes 262160 | tf_op jit(solution)/shard_map/psum | solution.py:57
  (101 shorter events, 72.8 us)
Async XLA Ops:
  7.2 487.6 %all-reduce.2.cloned.1.call-start = ((), (), s32[]{:S(2)}) async-start(), calls=%async_computation | async-start | bytes 524288 | tf_op jit(solution)/shard_map/psum | solution.py:57
  10.7 15.3 %collective-permute-start = (bf16[2,64,256]{2,1,0:T(8,128)(2,1)}, bf16[2,64,256]{2,1,0:T(8,128)(2,1)}, u32[]{:S(2)}, u32[]{:S(2)}) collective-permute-start(bf16[2,64,256]{2,1,0:T(8,128)(2,1)} %get-tuple-element.35), channel_id=1, source_target_pairs={{0,16},{16,32},{32,48},{48,64},{64,80},{80,96},{96,112},{112,128},... | collective-permute-start | bytes 196616 | tf_op jit(solution)/shard_map/ppermute | solution.py:16
  15.2 11.6 %collective-permute-start.1 = (bf16[2,64,256]{2,1,0:T(8,128)(2,1)}, bf16[2,64,256]{2,1,0:T(8,128)(2,1)}, u32[]{:S(2)}, u32[]{:S(2)}) collective-permute-start(bf16[2,64,256]{2,1,0:T(8,128)(2,1)} %get-tuple-element.34), channel_id=1, source_target_pairs={{16,0},{32,16},{48,32},{64,48},{80,64},{96,80},{112,96},{128,112},... | collective-permute-start | bytes 196616 | tf_op jit(solution)/shard_map/ppermute | solution.py:16
  17.8 9.9 %collective-permute-start.2 = (bf16[2,64,256]{2,1,0:T(8,128)(2,1)}, bf16[2,64,256]{2,1,0:T(8,128)(2,1)S(1)}, u32[]{:S(2)}, u32[]{:S(2)}) collective-permute-start(bf16[2,64,256]{2,1,0:T(8,128)(2,1)} %get-tuple-element.33), channel_id=1, source_target_pairs={{0,1},{1,2},{2,3},{3,4},{4,5},{5,6},{6,7},{7,8},{8,9},{9,10},{10,1... | collective-permute-start | bytes 196616 | tf_op jit(solution)/shard_map/ppermute | solution.py:16
  20.7 7.0 %collective-permute-start.3 = (bf16[2,64,256]{2,1,0:T(8,128)(2,1)}, bf16[2,64,256]{2,1,0:T(8,128)(2,1)S(1)}, u32[]{:S(2)}, u32[]{:S(2)}) collective-permute-start(bf16[2,64,256]{2,1,0:T(8,128)(2,1)} %get-tuple-element.32), channel_id=1, source_target_pairs={{1,0},{2,1},{3,2},{4,3},{5,4},{6,5},{7,6},{8,7},{9,8},{10,9},{11,1... | collective-permute-start | bytes 196616 | tf_op jit(solution)/shard_map/ppermute | solution.py:16
  46.6 11.4 %collective-permute-start.4 = (bf16[2,64,256]{2,1,0:T(8,128)(2,1)S(1)}, bf16[2,64,256]{2,1,0:T(8,128)(2,1)S(1)}, u32[]{:S(2)}, u32[]{:S(2)}) collective-permute-start(bf16[2,64,256]{2,1,0:T(8,128)(2,1)S(1)} %get-tuple-element.31), channel_id=1, source_target_pairs={{0,16},{16,32},{32,48},{48,64},{64,80},{80,96},{96,112},{112,128},... | collective-permute-start | bytes 196616 | tf_op jit(solution)/shard_map/ppermute | solution.py:16
  50.5 7.5 %collective-permute-start.5 = (bf16[2,64,256]{2,1,0:T(8,128)(2,1)S(1)}, bf16[2,64,256]{2,1,0:T(8,128)(2,1)S(1)}, u32[]{:S(2)}, u32[]{:S(2)}) collective-permute-start(bf16[2,64,256]{2,1,0:T(8,128)(2,1)S(1)} %get-tuple-element.30), channel_id=1, source_target_pairs={{16,0},{32,16},{48,32},{64,48},{80,64},{96,80},{112,96},{128,112},... | collective-permute-start | bytes 196616 | tf_op jit(solution)/shard_map/ppermute | solution.py:16
  52.5 5.6 %collective-permute-start.6 = (bf16[2,64,256]{2,1,0:T(8,128)(2,1)S(1)}, bf16[2,64,256]{2,1,0:T(8,128)(2,1)S(1)}, u32[]{:S(2)}, u32[]{:S(2)}) collective-permute-start(bf16[2,64,256]{2,1,0:T(8,128)(2,1)S(1)} %get-tuple-element.29), channel_id=1, source_target_pairs={{0,1},{1,2},{2,3},{3,4},{4,5},{5,6},{6,7},{7,8},{8,9},{9,10},{10,1... | collective-permute-start | bytes 196616 | tf_op jit(solution)/shard_map/ppermute | solution.py:16
  56.8 5.2 %collective-permute-start.7 = (bf16[2,64,256]{2,1,0:T(8,128)(2,1)S(1)}, bf16[2,64,256]{2,1,0:T(8,128)(2,1)S(1)}, u32[]{:S(2)}, u32[]{:S(2)}) collective-permute-start(bf16[2,64,256]{2,1,0:T(8,128)(2,1)S(1)} %get-tuple-element.28), channel_id=1, source_target_pairs={{1,0},{2,1},{3,2},{4,3},{5,4},{6,5},{7,6},{8,7},{9,8},{10,9},{11,1... | collective-permute-start | bytes 196616 | tf_op jit(solution)/shard_map/ppermute | solution.py:16
  81.5 12.9 %collective-permute-start.8 = (bf16[2,64,256]{2,1,0:T(8,128)(2,1)S(1)}, bf16[2,64,256]{2,1,0:T(8,128)(2,1)S(1)}, u32[]{:S(2)}, u32[]{:S(2)}) collective-permute-start(bf16[2,64,256]{2,1,0:T(8,128)(2,1)S(1)} %get-tuple-element.27), channel_id=1, source_target_pairs={{0,16},{16,32},{32,48},{48,64},{64,80},{80,96},{96,112},{112,128},... | collective-permute-start | bytes 196616 | tf_op jit(solution)/shard_map/ppermute | solution.py:16
  86.4 8.0 %collective-permute-start.9 = (bf16[2,64,256]{2,1,0:T(8,128)(2,1)S(1)}, bf16[2,64,256]{2,1,0:T(8,128)(2,1)S(1)}, u32[]{:S(2)}, u32[]{:S(2)}) collective-permute-start(bf16[2,64,256]{2,1,0:T(8,128)(2,1)S(1)} %get-tuple-element.26), channel_id=1, source_target_pairs={{16,0},{32,16},{48,32},{64,48},{80,64},{96,80},{112,96},{128,112},... | collective-permute-start | bytes 196616 | tf_op jit(solution)/shard_map/ppermute | solution.py:16
  88.3 6.1 %collective-permute-start.10 = (bf16[2,64,256]{2,1,0:T(8,128)(2,1)S(1)}, bf16[2,64,256]{2,1,0:T(8,128)(2,1)S(1)}, u32[]{:S(2)}, u32[]{:S(2)}) collective-permute-start(bf16[2,64,256]{2,1,0:T(8,128)(2,1)S(1)} %get-tuple-element.25), channel_id=1, source_target_pairs={{0,1},{1,2},{2,3},{3,4},{4,5},{5,6},{6,7},{7,8},{8,9},{9,10},{10,1... | collective-permute-start | bytes 196616 | tf_op jit(solution)/shard_map/ppermute | solution.py:16
  92.9 6.5 %collective-permute-start.11 = (bf16[2,64,256]{2,1,0:T(8,128)(2,1)S(1)}, bf16[2,64,256]{2,1,0:T(8,128)(2,1)S(1)}, u32[]{:S(2)}, u32[]{:S(2)}) collective-permute-start(bf16[2,64,256]{2,1,0:T(8,128)(2,1)S(1)} %get-tuple-element.24), channel_id=1, source_target_pairs={{1,0},{2,1},{3,2},{4,3},{5,4},{6,5},{7,6},{8,7},{9,8},{10,9},{11,1... | collective-permute-start | bytes 196616 | tf_op jit(solution)/shard_map/ppermute | solution.py:16
  119.3 12.9 %collective-permute-start.12 = (bf16[2,64,256]{2,1,0:T(8,128)(2,1)S(1)}, bf16[2,64,256]{2,1,0:T(8,128)(2,1)S(1)}, u32[]{:S(2)}, u32[]{:S(2)}) collective-permute-start(bf16[2,64,256]{2,1,0:T(8,128)(2,1)S(1)} %get-tuple-element.23), channel_id=1, source_target_pairs={{0,16},{16,32},{32,48},{48,64},{64,80},{80,96},{96,112},{112,128},... | collective-permute-start | bytes 196616 | tf_op jit(solution)/shard_map/ppermute | solution.py:16
  124.1 8.1 %collective-permute-start.13 = (bf16[2,64,256]{2,1,0:T(8,128)(2,1)S(1)}, bf16[2,64,256]{2,1,0:T(8,128)(2,1)S(1)}, u32[]{:S(2)}, u32[]{:S(2)}) collective-permute-start(bf16[2,64,256]{2,1,0:T(8,128)(2,1)S(1)} %get-tuple-element.22), channel_id=1, source_target_pairs={{16,0},{32,16},{48,32},{64,48},{80,64},{96,80},{112,96},{128,112},... | collective-permute-start | bytes 196616 | tf_op jit(solution)/shard_map/ppermute | solution.py:16
  126.1 6.2 %collective-permute-start.14 = (bf16[2,64,256]{2,1,0:T(8,128)(2,1)S(1)}, bf16[2,64,256]{2,1,0:T(8,128)(2,1)S(1)}, u32[]{:S(2)}, u32[]{:S(2)}) collective-permute-start(bf16[2,64,256]{2,1,0:T(8,128)(2,1)S(1)} %get-tuple-element.21), channel_id=1, source_target_pairs={{0,1},{1,2},{2,3},{3,4},{4,5},{5,6},{6,7},{7,8},{8,9},{9,10},{10,1... | collective-permute-start | bytes 196616 | tf_op jit(solution)/shard_map/ppermute | solution.py:16
  130.9 5.3 %collective-permute-start.15 = (bf16[2,64,256]{2,1,0:T(8,128)(2,1)S(1)}, bf16[2,64,256]{2,1,0:T(8,128)(2,1)S(1)}, u32[]{:S(2)}, u32[]{:S(2)}) collective-permute-start(bf16[2,64,256]{2,1,0:T(8,128)(2,1)S(1)} %get-tuple-element.20), channel_id=1, source_target_pairs={{1,0},{2,1},{3,2},{4,3},{5,4},{6,5},{7,6},{8,7},{9,8},{10,9},{11,1... | collective-permute-start | bytes 196616 | tf_op jit(solution)/shard_map/ppermute | solution.py:16
  156.1 11.9 %collective-permute-start.16 = (bf16[2,64,256]{2,1,0:T(8,128)(2,1)S(1)}, bf16[2,64,256]{2,1,0:T(8,128)(2,1)S(1)}, u32[]{:S(2)}, u32[]{:S(2)}) collective-permute-start(bf16[2,64,256]{2,1,0:T(8,128)(2,1)S(1)} %get-tuple-element.19), channel_id=1, source_target_pairs={{0,16},{16,32},{32,48},{48,64},{64,80},{80,96},{96,112},{112,128},... | collective-permute-start | bytes 196616 | tf_op jit(solution)/shard_map/ppermute | solution.py:16
  160.9 7.1 %collective-permute-start.17 = (bf16[2,64,256]{2,1,0:T(8,128)(2,1)S(1)}, bf16[2,64,256]{2,1,0:T(8,128)(2,1)S(1)}, u32[]{:S(2)}, u32[]{:S(2)}) collective-permute-start(bf16[2,64,256]{2,1,0:T(8,128)(2,1)S(1)} %get-tuple-element.18), channel_id=1, source_target_pairs={{16,0},{32,16},{48,32},{64,48},{80,64},{96,80},{112,96},{128,112},... | collective-permute-start | bytes 196616 | tf_op jit(solution)/shard_map/ppermute | solution.py:16
  162.9 5.2 %collective-permute-start.18 = (bf16[2,64,256]{2,1,0:T(8,128)(2,1)S(1)}, bf16[2,64,256]{2,1,0:T(8,128)(2,1)S(1)}, u32[]{:S(2)}, u32[]{:S(2)}) collective-permute-start(bf16[2,64,256]{2,1,0:T(8,128)(2,1)S(1)} %get-tuple-element.17), channel_id=1, source_target_pairs={{0,1},{1,2},{2,3},{3,4},{4,5},{5,6},{6,7},{7,8},{8,9},{9,10},{10,1... | collective-permute-start | bytes 196616 | tf_op jit(solution)/shard_map/ppermute | solution.py:16
  192.1 11.4 %collective-permute-start.20 = (bf16[2,64,256]{2,1,0:T(8,128)(2,1)}, bf16[2,64,256]{2,1,0:T(8,128)(2,1)}, u32[]{:S(2)}, u32[]{:S(2)}) collective-permute-start(bf16[2,64,256]{2,1,0:T(8,128)(2,1)} %get-tuple-element.15), channel_id=1, source_target_pairs={{0,16},{16,32},{32,48},{48,64},{64,80},{80,96},{96,112},{112,128},... | collective-permute-start | bytes 196616 | tf_op jit(solution)/shard_map/ppermute | solution.py:16
  197.4 7.0 %collective-permute-start.21 = (bf16[2,64,256]{2,1,0:T(8,128)(2,1)}, bf16[2,64,256]{2,1,0:T(8,128)(2,1)S(1)}, u32[]{:S(2)}, u32[]{:S(2)}) collective-permute-start(bf16[2,64,256]{2,1,0:T(8,128)(2,1)} %get-tuple-element.14), channel_id=1, source_target_pairs={{16,0},{32,16},{48,32},{64,48},{80,64},{96,80},{112,96},{128,112},... | collective-permute-start | bytes 196616 | tf_op jit(solution)/shard_map/ppermute | solution.py:16
  199.3 5.0 %collective-permute-start.22 = (bf16[2,64,256]{2,1,0:T(8,128)(2,1)}, bf16[2,64,256]{2,1,0:T(8,128)(2,1)S(1)}, u32[]{:S(2)}, u32[]{:S(2)}) collective-permute-start(bf16[2,64,256]{2,1,0:T(8,128)(2,1)} %get-tuple-element.13), channel_id=1, source_target_pairs={{0,1},{1,2},{2,3},{3,4},{4,5},{5,6},{6,7},{7,8},{8,9},{9,10},{10,1... | collective-permute-start | bytes 196616 | tf_op jit(solution)/shard_map/ppermute | solution.py:16
  202.2 5.2 %collective-permute-start.23 = (bf16[2,64,256]{2,1,0:T(8,128)(2,1)}, bf16[2,64,256]{2,1,0:T(8,128)(2,1)S(1)}, u32[]{:S(2)}, u32[]{:S(2)}) collective-permute-start(bf16[2,64,256]{2,1,0:T(8,128)(2,1)} %get-tuple-element.12), channel_id=1, source_target_pairs={{1,0},{2,1},{3,2},{4,3},{5,4},{6,5},{7,6},{8,7},{9,8},{10,9},{11,1... | collective-permute-start | bytes 196616 | tf_op jit(solution)/shard_map/ppermute | solution.py:16
  (6 other events, 86.7 us)
Sparse Core Ops, SparseCore 0:
  223.5 271.2 all-reduce.1
where the time goes:
time: 506 us; the launch traced here: 504 us
  waiting for transfers between devices  289 us (57%)
  local copies, waits for them, and re-layouts  78.9 us (16%)
  starting transfers between devices  71.4 us (14%)
  matrix products  47.8 us (9%)
  between operations  14.6 us (3%)
    psum x1, waiting for transfers between devices, on_device(): gram = lax.psum(local_gram, ('gx', 'gy'))  270 us
    ppermute x24, starting transfers between devices, from_behind(): lax.ppermute(value, axis, [(source, source + steps) for source in range(l...  71.4 us
    gather x6, local copies, waits for them, and re-layouts, scaled_apply(): gathered = extended[columns_of].reshape(blocks, -1, columns)  52 us
    dot_general x6, matrix products, scaled_apply(): jnp.einsum('rak,rkc->rac', couplings, gathered, preferred_element_type=jn...  43.8 us
    ppermute x24, waiting for transfers between devices, from_behind(): lax.ppermute(value, axis, [(source, source + steps) for source in range(l...  19.1 us
    gather x6, local copies, waits for them, and re-layouts, scaled_apply(): lowered[outgoing.reshape(-1)].reshape(4, halo_count, orbitals, columns)  14.2 us
  transfers between devices with their start and end apart: 25, of which 6 were waited for; matrix products, arithmetic and copies ran while one was open for 2% of the time, Pallas kernels for 0%

commit v1 on v0

v1 whole, which is shorter than its diff:
```python
import functools

import jax
import jax.numpy as jnp
from jax import lax
from jax.experimental import pallas as pl
from jax.experimental.pallas import tpu as pltpu
from jax.sharding import PartitionSpec as P

STEPS = 6
SHIFT = 0.1
HALF_WIDTH = 0.8

F32 = jnp.float32
BF16 = jnp.bfloat16
VMEM = pltpu.VMEM
SMEM = pltpu.SMEM

ORB = 64
NB = 8
BLK = 32
HB = 2
ROWS = BLK * ORB
SUB = 256
HALO = 4 * HB * ORB
WIDE = ROWS + HALO + 2 * ORB
SPARE = BLK + 4 * HB
MT = 512


def exchange_pairs(tiles_x, tiles_y):
    def at(i, j):
        return i * tiles_y + j

    def odd(i):
        return ((i - 1) ^ 1) + 1

    grid = [(i, j) for i in range(tiles_x) for j in range(tiles_y)]
    inner_x = [(at(i, j), at(i ^ 1, j)) for i, j in grid]
    inner_y = [(at(i, j), at(i, j ^ 1)) for i, j in grid]
    outer_x = [
        (at(i, j), at(i, j ^ 1) if i in (0, tiles_x - 1) else at(odd(i), j)) for i, j in grid
    ]
    outer_y = [
        (at(i, j), at(i ^ 1, j) if j in (0, tiles_y - 1) else at(i, odd(j))) for i, j in grid
    ]
    return inner_x, outer_x, inner_y, outer_y


def dot(a, b):
    return jnp.dot(a, b, preferred_element_type=F32)


def build_kernel(place, nbr, ham, sub, dense, base, cur, remap):
    for s in range(BLK):
        remap[s] = jnp.int32(s)
    for axis in range(2):
        pos, last = place[axis], place[2 + axis]
        parity = pos & 1
        for side in range(2):
            exists = (pos > 0) if side == 0 else (pos < last)
            op = jnp.where(parity == side, 1, 0) if side == 0 else jnp.where(parity == 0, 0, 1)
            for h in range(HB):
                s = BLK + (2 * axis + side) * HB + h
                remap[s] = jnp.where(exists, BLK + (2 * axis + op) * HB + h, SPARE)

    def clear(m, carry):
        dense[pl.ds(pl.multiple_of(m * ORB, ORB), ORB), :] = jnp.zeros((ORB, WIDE), BF16)
        return carry

    lax.fori_loop(0, BLK, clear, 0)
    low = lax.broadcasted_iota(jnp.int32, (ORB, 2 * ORB), 1) < ORB

    def row(r, carry):
        rows = pl.ds(pl.multiple_of(r * ORB, ORB), ORB)
        for kk in range(NB // 2):
            tile = ham[rows, kk * 128:(kk + 1) * 128].astype(F32)
            turned = pltpu.roll(tile, 64, 1)
            for e in range(2):
                s = remap[nbr[r, 2 * kk + e]]
                p = s & 1
                q = s >> 1
                high_part = jnp.where(low, 0.0, tile if e == 1 else turned)
                low_part = jnp.where(low, tile if e == 0 else turned, 0.0)
                piece = jnp.where(p == 0, low_part, high_part)
                cols = pl.ds(pl.multiple_of(q * 128, 128), 128)
                dense[rows, cols] = (dense[rows, cols].astype(F32) + piece).astype(BF16)
        return carry

    lax.fori_loop(0, BLK, row, 0)

    def local(m, carry):
        rows = pl.ds(pl.multiple_of(m * MT, MT), MT)
        wide = sub[rows, :].astype(F32)
        cur[rows, :] = wide
        product = dot(dense[rows, :ROWS], sub[...])
        base[rows, :] = (1.0 / HALF_WIDTH) * product - (SHIFT / HALF_WIDTH) * wide
        return carry

    lax.fori_loop(0, ROWS // MT, local, 0, unroll=True)


def first_packets_kernel(place, lists, sub, out_a, out_b, out_c, out_d):
    for n, out in enumerate((out_a, out_b, out_c, out_d)):
        parity = place[n // 2] & 1
        packet = 2 * (n // 2) + ((parity + n) & 1)
        for h in range(HB):
            b = lists[packet, h]
            out[h * ORB:(h + 1) * ORB, :] = sub[pl.ds(pl.multiple_of(b * ORB, ORB), ORB), :]


def packets_kernel(scale, place, lists, in_a, in_b, in_c, in_d, dense, base,
                   out_a, out_b, out_c, out_d, halo, rows_of, start):
    for n, got in enumerate((in_a, in_b, in_c, in_d)):
        halo[n * 2 * ORB:(n + 1) * 2 * ORB, :] = got[...]
    for n in range(4):
        parity = place[n // 2] & 1
        packet = 2 * (n // 2) + ((parity + n) & 1)
        for h in range(HB):
            at = pl.ds(pl.multiple_of(lists[packet, h] * ORB, ORB), ORB)
            here = slice((n * HB + h) * ORB, (n * HB + h + 1) * ORB)
            rows_of[here, :] = dense[at, ROWS:ROWS + HALO]
            start[here, :] = base[at, :]
    for n, out in enumerate((out_a, out_b, out_c, out_d)):
        here = slice(n * 2 * ORB, (n + 1) * 2 * ORB)
        out[...] = (start[here, :] + scale * dot(rows_of[here, :], halo[...])).astype(BF16)


def step_kernel(scale, in_a, in_b, in_c, in_d, dense, base, cur, new_cur, new_base, halo, low):
    for n, got in enumerate((in_a, in_b, in_c, in_d)):
        halo[n * 2 * ORB:(n + 1) * 2 * ORB, :] = got[...]

    def edge(m, carry):
        rows = pl.ds(pl.multiple_of(m * MT, MT), MT)
        value = base[rows, :] + scale * dot(dense[rows, ROWS:ROWS + HALO], halo[...])
        new_cur[rows, :] = value
        low[rows, :] = value.astype(BF16)
        return carry

    lax.fori_loop(0, ROWS // MT, edge, 0, unroll=True)

    def local(m, carry):
        rows = pl.ds(pl.multiple_of(m * MT, MT), MT)
        product = dot(dense[rows, :ROWS], low[...])
        new_base[rows, :] = (
            (2.0 / HALF_WIDTH) * product
            - (2.0 * SHIFT / HALF_WIDTH) * new_cur[rows, :]
            - cur[rows, :]
        )
        return carry

    lax.fori_loop(0, ROWS // MT, local, 0, unroll=True)


def last_kernel(scale, weight, in_a, in_b, in_c, in_d, dense, base, rotation, rotated, margin, halo, total):
    for n, got in enumerate((in_a, in_b, in_c, in_d)):
        halo[n * 2 * ORB:(n + 1) * 2 * ORB, :] = got[...]
    total[...] = jnp.zeros_like(total)

    def edge(m, carry):
        rows = pl.ds(pl.multiple_of(m * MT, MT), MT)
        value = base[rows, :] + scale * dot(dense[rows, ROWS:ROWS + HALO], halo[...])
        turned = dot(value.astype(BF16), rotation[...]).astype(BF16)
        rotated[rows, :] = turned
        total[...] += lax.dot_general(
            turned, turned, (((0,), (0,)), ((), ())), preferred_element_type=F32
        )
        return carry

    lax.fori_loop(0, ROWS // MT, edge, 0, unroll=True)
    margin[...] = (total[...] * weight).astype(BF16)


def params(**kw):
    return pltpu.CompilerParams(vmem_limit_bytes=16 * 1024 * 1024, **kw)


def cost(flops):
    return pl.CostEstimate(flops=int(flops), bytes_accessed=4 << 20, transcendentals=0)


V = pl.BlockSpec(memory_space=VMEM)
S = pl.BlockSpec(memory_space=SMEM)


def on_device(pairs, subspace, hamiltonian, neighbours, send_lists, rotation):
    ham = hamiltonian.reshape(ROWS, NB * ORB)
    nbr = neighbours.reshape(BLK, NB)
    lists = send_lists.reshape(4, HB)
    sub = subspace.reshape(ROWS, SUB)
    size_x, size_y = lax.axis_size("gx"), lax.axis_size("gy")
    place = jnp.stack([
        lax.axis_index("gx"), lax.axis_index("gy"), jnp.int32(size_x - 1), jnp.int32(size_y - 1)
    ]).astype(jnp.int32)

    packet = VMEM((2 * ORB, SUB), BF16)
    field = VMEM((ROWS, SUB), F32)
    halo = VMEM((HALO, SUB), BF16)

    def swap(packets):
        got = {}
        for n in (1, 3, 2, 0):
            got[n] = lax.ppermute(packets[n], ("gx", "gy"), pairs[n])
        return [got[n] for n in range(4)]

    packets = pl.pallas_call(
        first_packets_kernel,
        out_shape=[packet] * 4,
        in_specs=[S, S, V],
        out_specs=[V] * 4,
        compiler_params=params(),
        name="first_packets",
    )(place, lists, sub)
    received = swap(packets)
    dense, base, cur = pl.pallas_call(
        build_kernel,
        out_shape=[VMEM((ROWS, WIDE), BF16), field, field],
        in_specs=[S, S, V, V],
        out_specs=[V] * 3,
        scratch_shapes=[SMEM((SPARE + 8,), jnp.int32)],
        compiler_params=params(),
        cost_estimate=cost(2e9),
        name="build_and_local",
    )(place, nbr, ham, sub)
    for step in range(1, STEPS):
        scale = (1.0 if step == 1 else 2.0) / HALF_WIDTH
        packets = pl.pallas_call(
            functools.partial(packets_kernel, scale),
            out_shape=[packet] * 4,
            in_specs=[S, S] + [V] * 6,
            out_specs=[V] * 4,
            scratch_shapes=[halo, VMEM((HALO, HALO), BF16), VMEM((HALO, SUB), F32)],
            compiler_params=params(),
            name="packets",
        )(place, lists, *received, dense, base)
        landed = received
        received = swap(packets)
        cur, base = pl.pallas_call(
            functools.partial(step_kernel, scale),
            out_shape=[field, field],
            in_specs=[V] * 7,
            out_specs=[V] * 2,
            scratch_shapes=[halo, VMEM((ROWS, SUB), BF16)],
            compiler_params=params(),
            cost_estimate=cost(2.7e9),
            name="step",
        )(*landed, dense, base, cur)
    orbitals = ROWS * size_x * size_y
    rotated, share = pl.pallas_call(
        functools.partial(last_kernel, 2.0 / HALF_WIDTH, 1.0 / orbitals),
        out_shape=[jax.ShapeDtypeStruct((ROWS, SUB), BF16), VMEM((SUB, SUB), BF16)],
        in_specs=[V] * 7,
        out_specs=[V] * 2,
        scratch_shapes=[halo, VMEM((SUB, SUB), F32)],
        compiler_params=params(),
        name="last",
    )(*received, dense, base, rotation)
    parts = lax.all_to_all(share, ("gx", "gy"), 0, 0, tiled=True)
    margin = jnp.sum(parts.astype(F32), axis=0, keepdims=True)
    return rotated.reshape(subspace.shape), margin


def solution(mesh):
    pairs = exchange_pairs(mesh.shape["gx"], mesh.shape["gy"])
    return jax.shard_map(
        functools.partial(on_device, pairs),
        mesh=mesh,
        in_specs=(
            P("gx", "gy", None, None),
            P("gx", "gy", None, None, None),
            P("gx", "gy", None, None),
            P("gx", "gy", None, None),
            P(),
        ),
        out_specs=(P("gx", "gy", None, None), P(("gx", "gy"), None)),
        check_vma=False,
    )
```

time: 506 us -> 101 us (0.20)
  waiting for transfers between devices: 289 us -> 0.06 us
  local copies, waits for them, and re-layouts: 78.9 us -> 6.17 us
  matrix products: 47.8 us -> 0 us
  starting transfers between devices: 71.4 us -> 31.2 us
  Pallas kernels: 0 us -> 32.4 us
  blocking collectives: 0 us -> 28.7 us
  between operations: 14.6 us -> 0.93 us
    psum x1 -> x0, waiting for transfers between devices: 270 us -> none  [on_device(): gram = lax.psum(local_gram, ('gx', 'gy'))]
    gather x12 -> x0, local copies, waits for them, and re-layouts: 66.2 us -> none  [the longest x6 52 us: scaled_apply(): gathered = extended[columns_of].reshape(blocks, -1, columns)]
    dot_general x10 -> x0, matrix products: 47.8 us -> none  [the longest x6 43.8 us: scaled_apply(): jnp.einsum('rak,rkc->rac', couplings, gathered, preferred_element_type=jn...]
    ppermute x24, starting transfers between devices: 71.4 us -> 31.2 us  [swap(): got[n] = lax.ppermute(packets[n], ('gx', 'gy'), pairs[n])]
    pallas_call x0 -> x13, Pallas kernels: none -> 32.4 us  [the longest x5 16.3 us: on_device(): pl.pallas_call(functools.partial(step_kernel, scale), out_shape=[field, f...]
    all_to_all x0 -> x1, blocking collectives: none -> 28.7 us  [on_device(): parts = lax.all_to_all(share, ('gx', 'gy'), 0, 0, tiled=True)]
    ppermute x24, waiting for transfers between devices: 19.1 us -> 0.06 us  [swap(): got[n] = lax.ppermute(packets[n], ('gx', 'gy'), pairs[n])]
    slice x6 -> x0, local copies, waits for them, and re-layouts: 6.11 us -> none  [scaled_apply(): received.append(from_behind(packets[slot], 'gy', offset))]
  transfers between devices with their start and end apart: 25 -> 24, of which waited for: 6 -> 0; matrix products, arithmetic and copies ran while one was open for 2% -> 1% of each run, Pallas kernels for 0% -> 25%
where the time goes in v1:
time: 101 us
  Pallas kernels  32.4 us (32%)
  starting transfers between devices  31.2 us (31%)
  blocking collectives  28.7 us (28%)
  local copies, waits for them, and re-layouts  6.17 us (6%)
  other arithmetic  1.66 us (2%)
    ppermute x24, starting transfers between devices, swap(): got[n] = lax.ppermute(packets[n], ('gx', 'gy'), pairs[n])  31.2 us
    all_to_all x1, blocking collectives, on_device(): parts = lax.all_to_all(share, ('gx', 'gy'), 0, 0, tiled=True)  28.7 us
    pallas_call x5, Pallas kernels, on_device(): pl.pallas_call(functools.partial(step_kernel, scale), out_shape=[field, f...  16.3 us
    pallas_call x1, Pallas kernels, on_device(): pl.pallas_call(build_kernel, out_shape=[VMEM((ROWS, WIDE), BF16), field,...  8.49 us
    unnamed x11, local copies, waits for them, and re-layouts  4.89 us
    pallas_call x5, Pallas kernels, on_device(): pl.pallas_call(functools.partial(packets_kernel, scale), out_shape=[packe...  4.41 us
    pallas_call x1, Pallas kernels, on_device(): pl.pallas_call(functools.partial(last_kernel, 2.0 / HALF_WIDTH, 1.0 / orb...  2.61 us
  transfers between devices with their start and end apart: 24, of which 0 were waited for; matrix products, arithmetic and copies ran while one was open for 1% of the time, Pallas kernels for 25%

profile of v1, /device:TPU:1, one launch (start us, length us, event | category | flops | bytes accessed | tf_op | source)
XLA Modules:
  0.0 101.1 jit_solution(527088163178831816)
XLA Ops:
  1.5 1.2 %copy-done = bf16[1,1,2048,256]{3,2,1,0:T(8,128)(2,1)S(1)} copy-done((bf16[1,1,2048,256]{3,2,1,0:T(8,128)(2,1)S(1)}, bf16[1,1,2048,256]{3,2,1,0:T(8,128)(2,1)}, u32[]{:S(2)}) %copy-start) | copy-done | bytes 1048600
  3.3 3.3 %collective-permute-start = (bf16[128,256]{1,0:T(8,128)(2,1)S(1)}, bf16[128,256]{1,0:T(8,128)(2,1)S(1)}, u32[]{:S(2)}, u32[]{:S(2)}) collective-permute-start(bf16[128,256]{1,0:T(8,128)(2,1)S(1)} %get-tuple-element.40), channel_id=1, source_target_pairs={{0,16},{1,17},{2,18},{3,19},{4,20},{5,21},{6,22},{7,23},{8,24},{9,... | collective-permute-start | bytes 196616 | tf_op jit(solution)/shard_map/ppermute | solution.py:203
  6.6 1.1 %collective-permute-start.2 = (bf16[128,256]{1,0:T(8,128)(2,1)S(1)}, bf16[128,256]{1,0:T(8,128)(2,1)S(1)}, u32[]{:S(2)}, u32[]{:S(2)}) collective-permute-start(bf16[128,256]{1,0:T(8,128)(2,1)S(1)} %get-tuple-element.42), channel_id=1, source_target_pairs={{0,1},{1,0},{2,3},{3,2},{4,5},{5,4},{6,7},{7,6},{8,9},{9,8},{10,11... | collective-permute-start | bytes 196616 | tf_op jit(solution)/shard_map/ppermute | solution.py:203
  7.7 1.0 %collective-permute-start.3 = (bf16[128,256]{1,0:T(8,128)(2,1)S(1)}, bf16[128,256]{1,0:T(8,128)(2,1)S(1)}, u32[]{:S(2)}, u32[]{:S(2)}) collective-permute-start(bf16[128,256]{1,0:T(8,128)(2,1)S(1)} %get-tuple-element.43), channel_id=1, source_target_pairs={{0,16},{1,2},{2,1},{3,4},{4,3},{5,6},{6,5},{7,8},{8,7},{9,10},{10,... | collective-permute-start | bytes 196616 | tf_op jit(solution)/shard_map/ppermute | solution.py:203
  9.5 1.2 %copy-done.1 = bf16[1,1,2048,256]{3,2,1,0:T(8,128)(2,1)S(1)} copy-done((bf16[1,1,2048,256]{3,2,1,0:T(8,128)(2,1)S(1)}, bf16[1,1,2048,256]{3,2,1,0:T(8,128)(2,1)}, u32[]{:S(2)}) %copy-start.1) | copy-done | bytes 1048600
  10.8 1.6 %copy-done.3 = bf16[1,1,32,64,512]{4,3,2,1,0:T(8,128)(2,1)S(1)} copy-done((bf16[1,1,32,64,512]{4,3,2,1,0:T(8,128)(2,1)S(1)}, bf16[1,1,32,64,512]{4,3,2,1,0:T(8,128)(2,1)}, u32[]{:S(2)}) %copy-start.3) | copy-done | bytes 2097176
  12.3 8.5 %build_and_local.1 = (bf16[2048,2688]{1,0:T(8,128)(2,1)S(1)}, f32[2048,256]{1,0:T(8,128)S(1)}, f32[2048,256]{1,0:T(8,128)S(1)}) custom-call(s32[4]{0:T(128)S(1)} %pad_add_fusion.place, s32[32,8]{1,0:T(8,128)S(1)} %bitcast.12, bf16[2048,512]{1,0:T(8,128)(2,1)S(1)} %bitcast.13, bf16[2048,256]{1,0:T(8,128)(2,1)S(1)} %bitcast.10), custom_call_target="tpu_custom_call" | custom-call | flops 2000000000 | bytes 4194304 | tf_op jit(solution)/shard_map/build_and_local/pallas_call | solution.py:215
  22.5 3.2 %collective-permute-start.6 = (bf16[128,256]{1,0:T(8,128)(2,1)S(1)}, bf16[128,256]{1,0:T(8,128)(2,1)S(1)}, u32[]{:S(2)}, u32[]{:S(2)}) collective-permute-start(bf16[128,256]{1,0:T(8,128)(2,1)S(1)} %get-tuple-element.48), channel_id=1, source_target_pairs={{0,1},{1,0},{2,3},{3,2},{4,5},{5,4},{6,7},{7,6},{8,9},{9,8},{10,11... | collective-permute-start | bytes 196616 | tf_op jit(solution)/shard_map/ppermute | solution.py:203
  25.7 3.0 %step.5 = (f32[2048,256]{1,0:T(8,128)S(1)}, f32[2048,256]{1,0:T(8,128)S(1)}) custom-call(bf16[128,256]{1,0:T(8,128)(2,1)S(1)} %collective-permute-done.in_a, bf16[128,256]{1,0:T(8,128)(2,1)S(1)} %collective-permute-done.1.in_b, bf16[128,256]{1,0:T(8,128)(2,1)S(1)} %collective-permute-done.2.in_c, bf16[128,256]{1,0:T(8,128)(2,1)S(1)} %collective-permute-done.3.in_d, ...), custom_call_target="tpu_custom_call" | custom-call | flops 2700000000 | bytes 4194304 | tf_op jit(solution)/shard_map/step/pallas_call | solution.py:238
  29.6 3.7 %collective-permute-start.10 = (bf16[128,256]{1,0:T(8,128)(2,1)S(1)}, bf16[128,256]{1,0:T(8,128)(2,1)S(1)}, u32[]{:S(2)}, u32[]{:S(2)}) collective-permute-start(bf16[128,256]{1,0:T(8,128)(2,1)S(1)} %get-tuple-element.54), channel_id=1, source_target_pairs={{0,1},{1,0},{2,3},{3,2},{4,5},{5,4},{6,7},{7,6},{8,9},{9,8},{10,11... | collective-permute-start | bytes 196616 | tf_op jit(solution)/shard_map/ppermute | solution.py:203
  33.8 1.5 %collective-permute-start.9 = (bf16[128,256]{1,0:T(8,128)(2,1)S(1)}, bf16[128,256]{1,0:T(8,128)(2,1)S(1)}, u32[]{:S(2)}, u32[]{:S(2)}) collective-permute-start(bf16[128,256]{1,0:T(8,128)(2,1)S(1)} %get-tuple-element.53), channel_id=1, source_target_pairs={{0,1},{1,0},{2,3},{3,2},{4,5},{5,4},{6,7},{7,6},{8,9},{9,8},{10,11... | collective-permute-start | bytes 196616 | tf_op jit(solution)/shard_map/ppermute | solution.py:203
  35.3 3.0 %step.6 = (f32[2048,256]{1,0:T(8,128)S(1)}, f32[2048,256]{1,0:T(8,128)S(1)}) custom-call(bf16[128,256]{1,0:T(8,128)(2,1)S(1)} %collective-permute-done.4.in_a, bf16[128,256]{1,0:T(8,128)(2,1)S(1)} %collective-permute-done.5.in_b, bf16[128,256]{1,0:T(8,128)(2,1)S(1)} %collective-permute-done.6.in_c, bf16[128,256]{1,0:T(8,128)(2,1)S(1)} %collective-permute-done.7.in_d, ...), custom_call_target="tpu_custom_call" | custom-call | flops 2700000000 | bytes 4194304 | tf_op jit(solution)/shard_map/step/pallas_call | solution.py:238
  39.2 2.4 %collective-permute-start.12 = (bf16[128,256]{1,0:T(8,128)(2,1)S(1)}, bf16[128,256]{1,0:T(8,128)(2,1)S(1)}, u32[]{:S(2)}, u32[]{:S(2)}) collective-permute-start(bf16[128,256]{1,0:T(8,128)(2,1)S(1)} %get-tuple-element.58), channel_id=1, source_target_pairs={{0,16},{1,17},{2,18},{3,19},{4,20},{5,21},{6,22},{7,23},{8,24},{9,... | collective-permute-start | bytes 196616 | tf_op jit(solution)/shard_map/ppermute | solution.py:203
  41.9 1.5 %collective-permute-start.14 = (bf16[128,256]{1,0:T(8,128)(2,1)S(1)}, bf16[128,256]{1,0:T(8,128)(2,1)S(1)}, u32[]{:S(2)}, u32[]{:S(2)}) collective-permute-start(bf16[128,256]{1,0:T(8,128)(2,1)S(1)} %get-tuple-element.60), channel_id=1, source_target_pairs={{0,1},{1,0},{2,3},{3,2},{4,5},{5,4},{6,7},{7,6},{8,9},{9,8},{10,11... | collective-permute-start | bytes 196616 | tf_op jit(solution)/shard_map/ppermute | solution.py:203
  43.8 3.0 %step.7 = (f32[2048,256]{1,0:T(8,128)S(1)}, f32[2048,256]{1,0:T(8,128)S(1)}) custom-call(bf16[128,256]{1,0:T(8,128)(2,1)S(1)} %collective-permute-done.8.in_a, bf16[128,256]{1,0:T(8,128)(2,1)S(1)} %collective-permute-done.9.in_b, bf16[128,256]{1,0:T(8,128)(2,1)S(1)} %collective-permute-done.10.in_c, bf16[128,256]{1,0:T(8,128)(2,1)S(1)} %collective-permute-done.11.in_d, ...), custom_call_target="tpu_custom_call" | custom-call | flops 2700000000 | bytes 4194304 | tf_op jit(solution)/shard_map/step/pallas_call | solution.py:238
  48.2 2.6 %collective-permute-start.17 = (bf16[128,256]{1,0:T(8,128)(2,1)S(1)}, bf16[128,256]{1,0:T(8,128)(2,1)S(1)}, u32[]{:S(2)}, u32[]{:S(2)}) collective-permute-start(bf16[128,256]{1,0:T(8,128)(2,1)S(1)} %get-tuple-element.65), channel_id=1, source_target_pairs={{0,1},{1,0},{2,3},{3,2},{4,5},{5,4},{6,7},{7,6},{8,9},{9,8},{10,11... | collective-permute-start | bytes 196616 | tf_op jit(solution)/shard_map/ppermute | solution.py:203
  50.8 1.3 %collective-permute-start.18 = (bf16[128,256]{1,0:T(8,128)(2,1)S(1)}, bf16[128,256]{1,0:T(8,128)(2,1)S(1)}, u32[]{:S(2)}, u32[]{:S(2)}) collective-permute-start(bf16[128,256]{1,0:T(8,128)(2,1)S(1)} %get-tuple-element.66), channel_id=1, source_target_pairs={{0,1},{1,0},{2,3},{3,2},{4,5},{5,4},{6,7},{7,6},{8,9},{9,8},{10,11... | collective-permute-start | bytes 196616 | tf_op jit(solution)/shard_map/ppermute | solution.py:203
  52.1 3.0 %step.8 = (f32[2048,256]{1,0:T(8,128)S(1)}, f32[2048,256]{1,0:T(8,128)S(1)}) custom-call(bf16[128,256]{1,0:T(8,128)(2,1)S(1)} %collective-permute-done.12.in_a, bf16[128,256]{1,0:T(8,128)(2,1)S(1)} %collective-permute-done.13.in_b, bf16[128,256]{1,0:T(8,128)(2,1)S(1)} %collective-permute-done.14.in_c, bf16[128,256]{1,0:T(8,128)(2,1)S(1)} %collective-permute-done.15.in_d, ...), custom_call_target="tpu_custom_call" | custom-call | flops 2700000000 | bytes 4194304 | tf_op jit(solution)/shard_map/step/pallas_call | solution.py:238
  56.6 4.0 %collective-permute-start.21 = (bf16[128,256]{1,0:T(8,128)(2,1)S(1)}, bf16[128,256]{1,0:T(8,128)(2,1)S(1)}, u32[]{:S(2)}, u32[]{:S(2)}) collective-permute-start(bf16[128,256]{1,0:T(8,128)(2,1)S(1)} %get-tuple-element.71), channel_id=1, source_target_pairs={{0,1},{1,0},{2,3},{3,2},{4,5},{5,4},{6,7},{7,6},{8,9},{9,8},{10,11... | collective-permute-start | bytes 196616 | tf_op jit(solution)/shard_map/ppermute | solution.py:203
  60.6 2.7 %collective-permute-start.22 = (bf16[128,256]{1,0:T(8,128)(2,1)S(1)}, bf16[128,256]{1,0:T(8,128)(2,1)S(1)}, u32[]{:S(2)}, u32[]{:S(2)}) collective-permute-start(bf16[128,256]{1,0:T(8,128)(2,1)S(1)} %get-tuple-element.72), channel_id=1, source_target_pairs={{0,1},{1,0},{2,3},{3,2},{4,5},{5,4},{6,7},{7,6},{8,9},{9,8},{10,11... | collective-permute-start | bytes 196616 | tf_op jit(solution)/shard_map/ppermute | solution.py:203
  63.3 4.2 %step.9 = (f32[2048,256]{1,0:T(8,128)}, f32[2048,256]{1,0:T(8,128)S(1)}) custom-call(bf16[128,256]{1,0:T(8,128)(2,1)S(1)} %collective-permute-done.16.in_a, bf16[128,256]{1,0:T(8,128)(2,1)S(1)} %collective-permute-done.17.in_b, bf16[128,256]{1,0:T(8,128)(2,1)S(1)} %collective-permute-done.18.in_c, bf16[128,256]{1,0:T(8,128)(2,1)S(1)} %collective-permute-done.19.in_d, ...), custom_call_target="tpu_custom_call" | custom-call | flops 2700000000 | bytes 4194304 | tf_op jit(solution)/shard_map/step/pallas_call | solution.py:238
  67.6 2.6 %last.1 = (bf16[2048,256]{1,0:T(8,128)(2,1)}, bf16[256,256]{1,0:T(8,128)(2,1)S(1)}) custom-call(bf16[128,256]{1,0:T(8,128)(2,1)S(1)} %collective-permute-done.20.in_a, bf16[128,256]{1,0:T(8,128)(2,1)S(1)} %collective-permute-done.21.in_b, bf16[128,256]{1,0:T(8,128)(2,1)S(1)} %collective-permute-done.22.in_c, ...), custom_call_target="tpu_custom_call" | custom-call | tf_op jit(solution)/shard_map/last/pallas_call | solution.py:249
  71.5 28.7 %all_to_all.9 = bf16[256,2,128]{2,1,0:T(2,128)(2,1)S(1)} all-to-all(bf16[256,2,128]{2,1,0:T(2,128)(2,1)S(1)} %reshape.27), channel_id=1, replica_groups=mesh['gx'=16,'gy'=16] {'gx','gy'}, dimensions={0} | all-to-all | bytes 262144 | tf_op jit(solution)/shard_map/all_to_all | solution.py:258
  100.2 0.9 convert_reduce_fusion
  (55 shorter events, 10.9 us)
Async XLA Ops:
  3.3 17.5 %collective-permute-start = (bf16[128,256]{1,0:T(8,128)(2,1)S(1)}, bf16[128,256]{1,0:T(8,128)(2,1)S(1)}, u32[]{:S(2)}, u32[]{:S(2)}) collective-permute-start(bf16[128,256]{1,0:T(8,128)(2,1)S(1)} %get-tuple-element.40), channel_id=1, source_target_pairs={{0,16},{1,17},{2,18},{3,19},{4,20},{5,21},{6,22},{7,23},{8,24},{9,... | collective-permute-start | bytes 196616 | tf_op jit(solution)/shard_map/ppermute | solution.py:203
  6.6 14.2 %collective-permute-start.1 = (bf16[128,256]{1,0:T(8,128)(2,1)S(1)}, bf16[128,256]{1,0:T(8,128)(2,1)S(1)}, u32[]{:S(2)}, u32[]{:S(2)}) collective-permute-start(bf16[128,256]{1,0:T(8,128)(2,1)S(1)} %get-tuple-element.41), channel_id=1, source_target_pairs={{0,1},{1,0},{2,3},{3,2},{4,5},{5,4},{6,7},{7,6},{8,9},{9,8},{10,11... | collective-permute-start | bytes 196616 | tf_op jit(solution)/shard_map/ppermute | solution.py:203
  6.6 14.2 %collective-permute-start.2 = (bf16[128,256]{1,0:T(8,128)(2,1)S(1)}, bf16[128,256]{1,0:T(8,128)(2,1)S(1)}, u32[]{:S(2)}, u32[]{:S(2)}) collective-permute-start(bf16[128,256]{1,0:T(8,128)(2,1)S(1)} %get-tuple-element.42), channel_id=1, source_target_pairs={{0,1},{1,0},{2,3},{3,2},{4,5},{5,4},{6,7},{7,6},{8,9},{9,8},{10,11... | collective-permute-start | bytes 196616 | tf_op jit(solution)/shard_map/ppermute | solution.py:203
  7.7 13.1 %collective-permute-start.3 = (bf16[128,256]{1,0:T(8,128)(2,1)S(1)}, bf16[128,256]{1,0:T(8,128)(2,1)S(1)}, u32[]{:S(2)}, u32[]{:S(2)}) collective-permute-start(bf16[128,256]{1,0:T(8,128)(2,1)S(1)} %get-tuple-element.43), channel_id=1, source_target_pairs={{0,16},{1,2},{2,1},{3,4},{4,3},{5,6},{6,5},{7,8},{8,7},{9,10},{10,... | collective-permute-start | bytes 196616 | tf_op jit(solution)/shard_map/ppermute | solution.py:203
  21.8 6.9 %collective-permute-start.4 = (bf16[128,256]{1,0:T(8,128)(2,1)S(1)}, bf16[128,256]{1,0:T(8,128)(2,1)S(1)}, u32[]{:S(2)}, u32[]{:S(2)}) collective-permute-start(bf16[128,256]{1,0:T(8,128)(2,1)S(1)} %get-tuple-element.46), channel_id=1, source_target_pairs={{0,16},{1,17},{2,18},{3,19},{4,20},{5,21},{6,22},{7,23},{8,24},{9,... | collective-permute-start | bytes 196616 | tf_op jit(solution)/shard_map/ppermute | solution.py:203
  21.9 6.8 %collective-permute-start.5 = (bf16[128,256]{1,0:T(8,128)(2,1)S(1)}, bf16[128,256]{1,0:T(8,128)(2,1)S(1)}, u32[]{:S(2)}, u32[]{:S(2)}) collective-permute-start(bf16[128,256]{1,0:T(8,128)(2,1)S(1)} %get-tuple-element.47), channel_id=1, source_target_pairs={{0,1},{1,0},{2,3},{3,2},{4,5},{5,4},{6,7},{7,6},{8,9},{9,8},{10,11... | collective-permute-start | bytes 196616 | tf_op jit(solution)/shard_map/ppermute | solution.py:203
  22.5 6.2 %collective-permute-start.6 = (bf16[128,256]{1,0:T(8,128)(2,1)S(1)}, bf16[128,256]{1,0:T(8,128)(2,1)S(1)}, u32[]{:S(2)}, u32[]{:S(2)}) collective-permute-start(bf16[128,256]{1,0:T(8,128)(2,1)S(1)} %get-tuple-element.48), channel_id=1, source_target_pairs={{0,1},{1,0},{2,3},{3,2},{4,5},{5,4},{6,7},{7,6},{8,9},{9,8},{10,11... | collective-permute-start | bytes 196616 | tf_op jit(solution)/shard_map/ppermute | solution.py:203
  25.7 3.0 %collective-permute-start.7 = (bf16[128,256]{1,0:T(8,128)(2,1)S(1)}, bf16[128,256]{1,0:T(8,128)(2,1)S(1)}, u32[]{:S(2)}, u32[]{:S(2)}) collective-permute-start(bf16[128,256]{1,0:T(8,128)(2,1)S(1)} %get-tuple-element.49), channel_id=1, source_target_pairs={{0,16},{1,2},{2,1},{3,4},{4,3},{5,6},{6,5},{7,8},{8,7},{9,10},{10,... | collective-permute-start | bytes 196616 | tf_op jit(solution)/shard_map/ppermute | solution.py:203
  29.6 8.7 %collective-permute-start.10 = (bf16[128,256]{1,0:T(8,128)(2,1)S(1)}, bf16[128,256]{1,0:T(8,128)(2,1)S(1)}, u32[]{:S(2)}, u32[]{:S(2)}) collective-permute-start(bf16[128,256]{1,0:T(8,128)(2,1)S(1)} %get-tuple-element.54), channel_id=1, source_target_pairs={{0,1},{1,0},{2,3},{3,2},{4,5},{5,4},{6,7},{7,6},{8,9},{9,8},{10,11... | collective-permute-start | bytes 196616 | tf_op jit(solution)/shard_map/ppermute | solution.py:203
  33.3 5.0 %collective-permute-start.11 = (bf16[128,256]{1,0:T(8,128)(2,1)S(1)}, bf16[128,256]{1,0:T(8,128)(2,1)S(1)}, u32[]{:S(2)}, u32[]{:S(2)}) collective-permute-start(bf16[128,256]{1,0:T(8,128)(2,1)S(1)} %get-tuple-element.55), channel_id=1, source_target_pairs={{0,16},{1,2},{2,1},{3,4},{4,3},{5,6},{6,5},{7,8},{8,7},{9,10},{10,... | collective-permute-start | bytes 196616 | tf_op jit(solution)/shard_map/ppermute | solution.py:203
  33.3 5.0 %collective-permute-start.8 = (bf16[128,256]{1,0:T(8,128)(2,1)S(1)}, bf16[128,256]{1,0:T(8,128)(2,1)S(1)}, u32[]{:S(2)}, u32[]{:S(2)}) collective-permute-start(bf16[128,256]{1,0:T(8,128)(2,1)S(1)} %get-tuple-element.52), channel_id=1, source_target_pairs={{0,16},{1,17},{2,18},{3,19},{4,20},{5,21},{6,22},{7,23},{8,24},{9,... | collective-permute-start | bytes 196616 | tf_op jit(solution)/shard_map/ppermute | solution.py:203
  33.8 4.5 %collective-permute-start.9 = (bf16[128,256]{1,0:T(8,128)(2,1)S(1)}, bf16[128,256]{1,0:T(8,128)(2,1)S(1)}, u32[]{:S(2)}, u32[]{:S(2)}) collective-permute-start(bf16[128,256]{1,0:T(8,128)(2,1)S(1)} %get-tuple-element.53), channel_id=1, source_target_pairs={{0,1},{1,0},{2,3},{3,2},{4,5},{5,4},{6,7},{7,6},{8,9},{9,8},{10,11... | collective-permute-start | bytes 196616 | tf_op jit(solution)/shard_map/ppermute | solution.py:203
  39.2 7.6 %collective-permute-start.12 = (bf16[128,256]{1,0:T(8,128)(2,1)S(1)}, bf16[128,256]{1,0:T(8,128)(2,1)S(1)}, u32[]{:S(2)}, u32[]{:S(2)}) collective-permute-start(bf16[128,256]{1,0:T(8,128)(2,1)S(1)} %get-tuple-element.58), channel_id=1, source_target_pairs={{0,16},{1,17},{2,18},{3,19},{4,20},{5,21},{6,22},{7,23},{8,24},{9,... | collective-permute-start | bytes 196616 | tf_op jit(solution)/shard_map/ppermute | solution.py:203
  41.6 5.2 %collective-permute-start.13 = (bf16[128,256]{1,0:T(8,128)(2,1)S(1)}, bf16[128,256]{1,0:T(8,128)(2,1)S(1)}, u32[]{:S(2)}, u32[]{:S(2)}) collective-permute-start(bf16[128,256]{1,0:T(8,128)(2,1)S(1)} %get-tuple-element.59), channel_id=1, source_target_pairs={{0,1},{1,0},{2,3},{3,2},{4,5},{5,4},{6,7},{7,6},{8,9},{9,8},{10,11... | collective-permute-start | bytes 196616 | tf_op jit(solution)/shard_map/ppermute | solution.py:203
  41.9 4.9 %collective-permute-start.14 = (bf16[128,256]{1,0:T(8,128)(2,1)S(1)}, bf16[128,256]{1,0:T(8,128)(2,1)S(1)}, u32[]{:S(2)}, u32[]{:S(2)}) collective-permute-start(bf16[128,256]{1,0:T(8,128)(2,1)S(1)} %get-tuple-element.60), channel_id=1, source_target_pairs={{0,1},{1,0},{2,3},{3,2},{4,5},{5,4},{6,7},{7,6},{8,9},{9,8},{10,11... | collective-permute-start | bytes 196616 | tf_op jit(solution)/shard_map/ppermute | solution.py:203
  43.4 3.4 %collective-permute-start.15 = (bf16[128,256]{1,0:T(8,128)(2,1)S(1)}, bf16[128,256]{1,0:T(8,128)(2,1)S(1)}, u32[]{:S(2)}, u32[]{:S(2)}) collective-permute-start(bf16[128,256]{1,0:T(8,128)(2,1)S(1)} %get-tuple-element.61), channel_id=1, source_target_pairs={{0,16},{1,2},{2,1},{3,4},{4,3},{5,6},{6,5},{7,8},{8,7},{9,10},{10,... | collective-permute-start | bytes 196616 | tf_op jit(solution)/shard_map/ppermute | solution.py:203
  47.8 7.3 %collective-permute-start.16 = (bf16[128,256]{1,0:T(8,128)(2,1)S(1)}, bf16[128,256]{1,0:T(8,128)(2,1)S(1)}, u32[]{:S(2)}, u32[]{:S(2)}) collective-permute-start(bf16[128,256]{1,0:T(8,128)(2,1)S(1)} %get-tuple-element.64), channel_id=1, source_target_pairs={{0,16},{1,17},{2,18},{3,19},{4,20},{5,21},{6,22},{7,23},{8,24},{9,... | collective-permute-start | bytes 196616 | tf_op jit(solution)/shard_map/ppermute | solution.py:203
  48.2 6.9 %collective-permute-start.17 = (bf16[128,256]{1,0:T(8,128)(2,1)S(1)}, bf16[128,256]{1,0:T(8,128)(2,1)S(1)}, u32[]{:S(2)}, u32[]{:S(2)}) collective-permute-start(bf16[128,256]{1,0:T(8,128)(2,1)S(1)} %get-tuple-element.65), channel_id=1, source_target_pairs={{0,1},{1,0},{2,3},{3,2},{4,5},{5,4},{6,7},{7,6},{8,9},{9,8},{10,11... | collective-permute-start | bytes 196616 | tf_op jit(solution)/shard_map/ppermute | solution.py:203
  50.8 4.3 %collective-permute-start.18 = (bf16[128,256]{1,0:T(8,128)(2,1)S(1)}, bf16[128,256]{1,0:T(8,128)(2,1)S(1)}, u32[]{:S(2)}, u32[]{:S(2)}) collective-permute-start(bf16[128,256]{1,0:T(8,128)(2,1)S(1)} %get-tuple-element.66), channel_id=1, source_target_pairs={{0,1},{1,0},{2,3},{3,2},{4,5},{5,4},{6,7},{7,6},{8,9},{9,8},{10,11... | collective-permute-start | bytes 196616 | tf_op jit(solution)/shard_map/ppermute | solution.py:203
  52.0 3.1 %collective-permute-start.19 = (bf16[128,256]{1,0:T(8,128)(2,1)S(1)}, bf16[128,256]{1,0:T(8,128)(2,1)S(1)}, u32[]{:S(2)}, u32[]{:S(2)}) collective-permute-start(bf16[128,256]{1,0:T(8,128)(2,1)S(1)} %get-tuple-element.67), channel_id=1, source_target_pairs={{0,16},{1,2},{2,1},{3,4},{4,3},{5,6},{6,5},{7,8},{8,7},{9,10},{10,... | collective-permute-start | bytes 196616 | tf_op jit(solution)/shard_map/ppermute | solution.py:203
  56.0 11.6 %collective-permute-start.20 = (bf16[128,256]{1,0:T(8,128)(2,1)S(1)}, bf16[128,256]{1,0:T(8,128)(2,1)S(1)}, u32[]{:S(2)}, u32[]{:S(2)}) collective-permute-start(bf16[128,256]{1,0:T(8,128)(2,1)S(1)} %get-tuple-element.70), channel_id=1, source_target_pairs={{0,16},{1,17},{2,18},{3,19},{4,20},{5,21},{6,22},{7,23},{8,24},{9,... | collective-permute-start | bytes 196616 | tf_op jit(solution)/shard_map/ppermute | solution.py:203
  56.6 11.0 %collective-permute-start.21 = (bf16[128,256]{1,0:T(8,128)(2,1)S(1)}, bf16[128,256]{1,0:T(8,128)(2,1)S(1)}, u32[]{:S(2)}, u32[]{:S(2)}) collective-permute-start(bf16[128,256]{1,0:T(8,128)(2,1)S(1)} %get-tuple-element.71), channel_id=1, source_target_pairs={{0,1},{1,0},{2,3},{3,2},{4,5},{5,4},{6,7},{7,6},{8,9},{9,8},{10,11... | collective-permute-start | bytes 196616 | tf_op jit(solution)/shard_map/ppermute | solution.py:203
  60.6 7.0 %collective-permute-start.22 = (bf16[128,256]{1,0:T(8,128)(2,1)S(1)}, bf16[128,256]{1,0:T(8,128)(2,1)S(1)}, u32[]{:S(2)}, u32[]{:S(2)}) collective-permute-start(bf16[128,256]{1,0:T(8,128)(2,1)S(1)} %get-tuple-element.72), channel_id=1, source_target_pairs={{0,1},{1,0},{2,3},{3,2},{4,5},{5,4},{6,7},{7,6},{8,9},{9,8},{10,11... | collective-permute-start | bytes 196616 | tf_op jit(solution)/shard_map/ppermute | solution.py:203
  63.3 4.3 %collective-permute-start.23 = (bf16[128,256]{1,0:T(8,128)(2,1)S(1)}, bf16[128,256]{1,0:T(8,128)(2,1)S(1)}, u32[]{:S(2)}, u32[]{:S(2)}) collective-permute-start(bf16[128,256]{1,0:T(8,128)(2,1)S(1)} %get-tuple-element.73), channel_id=1, source_target_pairs={{0,16},{1,2},{2,1},{3,4},{4,3},{5,6},{6,5},{7,8},{8,7},{9,10},{10,... | collective-permute-start | bytes 196616 | tf_op jit(solution)/shard_map/ppermute | solution.py:203
  (4 other events, 8.3 us)

commit v2 on v1

v2 whole, which is shorter than its diff:
```python
import functools

import jax
import jax.numpy as jnp
from jax import lax
from jax.experimental import pallas as pl
from jax.experimental.pallas import tpu as pltpu
from jax.sharding import PartitionSpec as P

STEPS = 6
SHIFT = 0.1
HALF_WIDTH = 0.8

F32 = jnp.float32
BF16 = jnp.bfloat16
VMEM = pltpu.VMEM
SMEM = pltpu.SMEM

ORB = 64
NB = 8
BLK = 32
HB = 2
ROWS = BLK * ORB
SUB = 256
HALO = 4 * HB * ORB
WIDE = ROWS + HALO + 2 * ORB
SPARE = BLK + 4 * HB
MT = 512
GROUP = 4


SWAPS = ((0, 1), (1, 1), (1, 0), (0, 0))


def exchange_pairs(tiles):
    grid = [(i, j) for i in range(tiles[0]) for j in range(tiles[1])]

    def partner(spot, axis, outer):
        place = list(spot)
        if outer and place[axis] in (0, tiles[axis] - 1):
            place[1 - axis] ^= 1
        else:
            place[axis] = ((place[axis] - outer) ^ 1) + outer
        return place[0] * tiles[1] + place[1]

    return [[(i * tiles[1] + j, partner((i, j), *swap)) for i, j in grid] for swap in SWAPS]


def dot(a, b):
    return jnp.dot(a, b, preferred_element_type=F32)


def build_kernel(meta, nbr, ham, sub, cleared, dense, base, cur, remap):
    for s in range(BLK):
        remap[s] = jnp.int32(s)
    for axis in range(2):
        pos, last = meta[axis], meta[2 + axis]
        even = (pos & 1) == 0
        inner, outer = SWAPS.index((axis, 0)), SWAPS.index((axis, 1))
        before, after = jnp.where(even, outer, inner), jnp.where(even, inner, outer)
        for h in range(HB):
            s = BLK + 2 * axis * HB + h
            remap[s] = jnp.where(pos > 0, BLK + before * HB + h, SPARE)
            remap[s + HB] = jnp.where(pos < last, BLK + after * HB + h, SPARE)

    low = lax.broadcasted_iota(jnp.int32, (ORB, 2 * ORB), 1) < ORB
    keep_low = jnp.where(low, 1.0, 0.0).astype(BF16)
    keep_high = jnp.where(low, 0.0, 1.0).astype(BF16)

    def group(g, carry):
        rows = [pl.ds(pl.multiple_of((g * GROUP + n) * ORB, ORB), ORB) for n in range(GROUP)]
        for kk in range(NB // 2):
            tiles = [ham[rows[n], kk * 128:(kk + 1) * 128] for n in range(GROUP)]
            turned = [pltpu.roll(tile, 64, 1) for tile in tiles]
            for e in range(2):
                spots, values = [], []
                for n in range(GROUP):
                    s = remap[nbr[2 * kk + e, g * GROUP + n]]
                    kept, moved = (keep_low, keep_high) if e == 0 else (keep_high, keep_low)
                    piece = jnp.where((s & 1) == e, tiles[n] * kept, turned[n] * moved)
                    spots.append((rows[n], pl.ds(pl.multiple_of((s >> 1) * 128, 128), 128)))
                    values.append(dense[spots[n]] + piece)
                for n in range(GROUP):
                    dense[spots[n]] = values[n]
        return carry

    lax.fori_loop(0, BLK // GROUP, group, 0)
    for m in range(ROWS // MT):
        rows = slice(m * MT, (m + 1) * MT)
        wide = sub[rows, :].astype(F32)
        cur[rows, :] = wide
        product = dot(dense[rows, :ROWS], sub[...])
        base[rows, :] = (1.0 / HALF_WIDTH) * product - (SHIFT / HALF_WIDTH) * wide


def sent_rows(meta, n, h):
    axis, outer = SWAPS[n]
    packet = 2 * axis + ((meta[axis] + outer) & 1)
    return pl.ds(pl.multiple_of(meta[4 + h * 4 + packet] * ORB, ORB), ORB)


def first_kernel(limits, lists, nbr_hbm, ham_hbm, sub_hbm, out_a, out_b, out_c, out_d, meta, nbr, ham, sub, dense, sems):
    for axis, name in enumerate(("gx", "gy")):
        meta[axis] = lax.axis_index(name)
        meta[2 + axis] = jnp.int32(limits[axis])
    for n in range(4):
        for h in range(HB):
            meta[4 + h * 4 + n] = lists[h, n]
    copies = []
    for n, out in enumerate((out_a, out_b, out_c, out_d)):
        for h in range(HB):
            copies.append((sub_hbm.at[sent_rows(meta, n, h), :], out.at[pl.ds(h * ORB, ORB), :]))
    copies += [(nbr_hbm, nbr), (ham_hbm, ham), (sub_hbm, sub)]
    copies = [pltpu.make_async_copy(*pair, sems.at[n]) for n, pair in enumerate(copies)]
    for copy in copies:
        copy.start()

    def clear(m, carry):
        dense[pl.ds(pl.multiple_of(m * ORB, ORB), ORB), :ROWS + HALO] = jnp.zeros((ORB, ROWS + HALO), BF16)
        return carry

    lax.fori_loop(0, BLK, clear, 0)
    for copy in copies:
        copy.wait()


def packets_kernel(scale, meta, in_a, in_b, in_c, in_d, dense, base, out_a, out_b, out_c, out_d):
    outs = (out_a, out_b, out_c, out_d)
    halo = jnp.concatenate([got[...] for got in (in_a, in_b, in_c, in_d)], axis=0)
    spots = [sent_rows(meta, n, h) for n in range(4) for h in range(HB)]
    rows_of = jnp.concatenate([dense[at, ROWS:ROWS + HALO] for at in spots], axis=0)
    product = dot(rows_of, halo)
    for n, at in enumerate(spots):
        here = slice(n * ORB, (n + 1) * ORB)
        out = outs[n // HB]
        out[n % HB * ORB:(n % HB + 1) * ORB, :] = (base[at, :] + scale * product[here, :]).astype(BF16)


def step_kernel(scale, in_a, in_b, in_c, in_d, dense, base, before, new_base, cur, halo, low):
    for n, got in enumerate((in_a, in_b, in_c, in_d)):
        halo[n * 2 * ORB:(n + 1) * 2 * ORB, :] = got[...]
    for m in range(ROWS // MT):
        rows = slice(m * MT, (m + 1) * MT)
        value = base[rows, :] + scale * dot(dense[rows, ROWS:ROWS + HALO], halo[...])
        cur[rows, :] = value
        low[rows, :] = value.astype(BF16)
    for m in range(ROWS // MT):
        rows = slice(m * MT, (m + 1) * MT)
        product = dot(dense[rows, :ROWS], low[...])
        new_base[rows, :] = (
            (2.0 / HALF_WIDTH) * product
            - (2.0 * SHIFT / HALF_WIDTH) * cur[rows, :]
            - before[rows, :]
        )


def last_kernel(scale, weight, in_a, in_b, in_c, in_d, dense, base, rotation, rotated, margin, halo, total):
    for n, got in enumerate((in_a, in_b, in_c, in_d)):
        halo[n * 2 * ORB:(n + 1) * 2 * ORB, :] = got[...]
    for m in range(ROWS // MT):
        rows = slice(m * MT, (m + 1) * MT)
        value = base[rows, :] + scale * dot(dense[rows, ROWS:ROWS + HALO], halo[...])
        turned = dot(value.astype(BF16), rotation[...]).astype(BF16)
        rotated[rows, :] = turned
        share = lax.dot_general(turned, turned, (((0,), (0,)), ((), ())), preferred_element_type=F32)
        total[...] = share if m == 0 else total[...] + share
    margin[...] = (total[...] * weight).reshape(SUB, 2, SUB // 2).astype(BF16)


def sum_kernel(parts, out):
    total = jnp.sum(parts[...].astype(F32), axis=0)
    for n in range(2):
        out[:, n * 128:(n + 1) * 128] = total[n:n + 1, :]


def params(**kw):
    return pltpu.CompilerParams(vmem_limit_bytes=16 * 1024 * 1024, **kw)


def cost(flops):
    return pl.CostEstimate(flops=int(flops), bytes_accessed=4 << 20, transcendentals=0)


V = pl.BlockSpec(memory_space=VMEM)
S = pl.BlockSpec(memory_space=SMEM)
H = pl.BlockSpec(memory_space=pltpu.HBM)


def on_device(pairs, subspace, hamiltonian, neighbours, send_lists, rotation):
    ham = hamiltonian.reshape(ROWS, NB * ORB)
    nbr = neighbours.reshape(BLK, NB).T
    lists = send_lists.reshape(4, HB).T
    sub = subspace.reshape(ROWS, SUB)
    ham, sub, nbr = [pltpu.with_memory_space_constraint(x, pltpu.HBM) for x in (ham, sub, nbr)]
    size_x, size_y = lax.axis_size("gx"), lax.axis_size("gy")
    packet = VMEM((2 * ORB, SUB), BF16)
    field = VMEM((ROWS, SUB), F32)
    halo = VMEM((HALO, SUB), BF16)

    def swap(packets):
        return [lax.ppermute(packets[n], ("gx", "gy"), pairs[n]) for n in range(4)]

    table = VMEM((ROWS, WIDE), BF16)
    *packets, meta, nbr, ham, sub, dense = pl.pallas_call(
        functools.partial(first_kernel, (size_x - 1, size_y - 1)),
        out_shape=[packet] * 4 + [
            SMEM((4 + 4 * HB,), jnp.int32), SMEM(nbr.shape, jnp.int32), VMEM(ham.shape, BF16), VMEM(sub.shape, BF16), table
        ],
        in_specs=[S, H, H, H],
        out_specs=[V] * 4 + [S, S, V, V, V],
        scratch_shapes=[pltpu.SemaphoreType.DMA((4 * HB + 3,))],
        compiler_params=params(),
        name="first",
    )(lists, nbr, ham, sub)
    received = swap(packets)
    dense, base, *cur = pl.pallas_call(
        build_kernel,
        out_shape=[table, field, field],
        in_specs=[S, S, V, V, V],
        out_specs=[V] * 3,
        input_output_aliases={4: 0},
        scratch_shapes=[SMEM((SPARE + 8,), jnp.int32)],
        compiler_params=params(),
        cost_estimate=cost(2e9),
        name="build_and_local",
    )(meta, nbr, ham, sub, dense)
    for step in range(1, STEPS):
        scale = (1.0 if step == 1 else 2.0) / HALF_WIDTH
        packets = pl.pallas_call(
            functools.partial(packets_kernel, scale),
            out_shape=[packet] * 4,
            in_specs=[S] + [V] * 6,
            out_specs=[V] * 4,
            compiler_params=params(),
            name="packets",
        )(meta, *received, dense, base)
        landed = received
        received = swap(packets)
        keep = step < STEPS - 1
        fields = [VMEM((ROWS, SUB), F32)] * (2 if keep else 1)
        base, *cur = pl.pallas_call(
            functools.partial(step_kernel, scale),
            out_shape=fields,
            in_specs=[V] * 7,
            out_specs=[V] * len(fields),
            scratch_shapes=([] if keep else [field]) + [halo, VMEM((ROWS, SUB), BF16)],
            compiler_params=params(),
            cost_estimate=cost(2.7e9),
            name="step",
        )(*landed, dense, base, *cur)
    orbitals = ROWS * size_x * size_y
    rotated, share = pl.pallas_call(
        functools.partial(last_kernel, 2.0 / HALF_WIDTH, 1.0 / orbitals),
        out_shape=[VMEM((ROWS, SUB), BF16), VMEM((SUB, 2, SUB // 2), BF16)],
        in_specs=[V] * 7,
        out_specs=[V] * 2,
        scratch_shapes=[halo, VMEM((SUB, SUB), F32)],
        compiler_params=params(),
        name="last",
    )(*received, dense, base, rotation)
    parts = lax.all_to_all(share, ("gx", "gy"), 0, 0, tiled=True)
    margin = pl.pallas_call(
        sum_kernel,
        out_shape=jax.ShapeDtypeStruct((1, SUB), F32),
        in_specs=[V],
        out_specs=V,
        compiler_params=params(),
        name="sum_parts",
    )(parts)
    return rotated.reshape(subspace.shape), margin


def solution(mesh):
    pairs = exchange_pairs((mesh.shape["gx"], mesh.shape["gy"]))
    return jax.shard_map(
        functools.partial(on_device, pairs),
        mesh=mesh,
        in_specs=(
            P("gx", "gy", None, None),
            P("gx", "gy", None, None, None),
            P("gx", "gy", None, None),
            P("gx", "gy", None, None),
            P(),
        ),
        out_specs=(P("gx", "gy", None, None), P(("gx", "gy"), None)),
        check_vma=False,
    )
```

time: 101 us -> 88 us (0.87)
  blocking collectives: 28.7 us -> 0 us
  starting transfers between devices: 31.2 us -> 46.4 us
  waiting for transfers between devices: 0.06 us -> 12.2 us
  Pallas kernels: 32.4 us -> 26.7 us
  local copies, waits for them, and re-layouts: 6.17 us -> 1.65 us
  other arithmetic: 1.66 us -> 0 us
    all_to_all x1 -> x0, blocking collectives: 28.7 us -> none  [on_device(): parts = lax.all_to_all(share, ('gx', 'gy'), 0, 0, tiled=True)]
    all_to_all x0 -> x1, starting transfers between devices: none -> 14.7 us  [on_device(): parts = lax.all_to_all(share, ('gx', 'gy'), 0, 0, tiled=True)]
    all_to_all x0 -> x1, waiting for transfers between devices: none -> 12.2 us  [on_device(): parts = lax.all_to_all(share, ('gx', 'gy'), 0, 0, tiled=True)]
    unnamed x11 -> x5, local copies, waits for them, and re-layouts: 4.89 us -> 1.65 us
    pallas_call x5, Pallas kernels: 4.41 us -> 1.5 us  [on_device(): pl.pallas_call(functools.partial(packets_kernel, scale), out_shape=[packe...]
    pallas_call x7 -> x8, Pallas kernels: 25.4 us -> 22.6 us  [the longest x5 14.6 us: on_device(): pl.pallas_call(functools.partial(step_kernel, scale), out_shape=fields, i...]
  transfers between devices with their start and end apart: 24 -> 25, of which waited for: 0 -> 1; matrix products, arithmetic and copies ran while one was open for 1% -> 1% of each run, Pallas kernels for 25% -> 22%
where the time goes in v2:
time: 88 us; the launch traced here: 87.9 us
  starting transfers between devices  46.4 us (53%)
  Pallas kernels  26.7 us (30%)
  waiting for transfers between devices  12.2 us (14%)
  local copies, waits for them, and re-layouts  1.65 us (2%)
  between operations  0.95 us (1%)
    ppermute x24, starting transfers between devices, swap(): return [lax.ppermute(packets[n], ('gx', 'gy'), pairs[n]) for n in range(4)]  31.6 us
    all_to_all x1, starting transfers between devices, on_device(): parts = lax.all_to_all(share, ('gx', 'gy'), 0, 0, tiled=True)  14.7 us
    pallas_call x5, Pallas kernels, on_device(): pl.pallas_call(functools.partial(step_kernel, scale), out_shape=fields, i...  14.6 us
    all_to_all x1, waiting for transfers between devices, on_device(): parts = lax.all_to_all(share, ('gx', 'gy'), 0, 0, tiled=True)  12.2 us
    pallas_call x1, Pallas kernels, on_device(): pl.pallas_call(build_kernel, out_shape=[table, field, field], in_specs=[S...  4.53 us
    pallas_call x1, Pallas kernels, on_device(): pl.pallas_call(functools.partial(first_kernel, (size_x - 1, size_y - 1)),...  2.67 us
    pallas_call x1, Pallas kernels, on_device(): pl.pallas_call(functools.partial(last_kernel, 2.0 / HALF_WIDTH, 1.0 / orb...  2.54 us
  transfers between devices with their start and end apart: 25, of which 1 were waited for; matrix products, arithmetic and copies ran while one was open for 1% of the time, Pallas kernels for 22%

profile of v2, /device:TPU:1, one launch (start us, length us, event | category | flops | bytes accessed | tf_op | source)
XLA Modules:
  0.0 87.9 jit_solution(9689838026844931620)
XLA Ops:
  1.3 2.7 %first.1 = (bf16[128,256]{1,0:T(8,128)(2,1)S(1)}, bf16[128,256]{1,0:T(8,128)(2,1)S(1)}, bf16[128,256]{1,0:T(8,128)(2,1)S(1)}, bf16[128,256]{1,0:T(8,128)(2,1)S(1...) custom-call(s32[2,4]{1,0:T(2,128)S(1)} %bitcast.10, ...), custom_call_target="tpu_custom_call" | custom-call | tf_op jit(solution)/shard_map/first/pallas_call | solution.py:204
  4.0 2.7 %collective-permute-start = (bf16[128,256]{1,0:T(8,128)(2,1)S(1)}, bf16[128,256]{1,0:T(8,128)(2,1)S(1)}, u32[]{:S(2)}, u32[]{:S(2)}) collective-permute-start(bf16[128,256]{1,0:T(8,128)(2,1)S(1)} %get-tuple-element.45), channel_id=1, source_target_pairs={{0,1},{1,0},{2,3},{3,2},{4,5},{5,4},{6,7},{7,6},{8,9},{9,8},{10,11... | collective-permute-start | bytes 196616 | tf_op jit(solution)/shard_map/ppermute | solution.py:201
  7.5 2.4 %collective-permute-start.2 = (bf16[128,256]{1,0:T(8,128)(2,1)S(1)}, bf16[128,256]{1,0:T(8,128)(2,1)S(1)}, u32[]{:S(2)}, u32[]{:S(2)}) collective-permute-start(bf16[128,256]{1,0:T(8,128)(2,1)S(1)} %get-tuple-element.47), channel_id=1, source_target_pairs={{0,1},{1,0},{2,3},{3,2},{4,5},{5,4},{6,7},{7,6},{8,9},{9,8},{10,11... | collective-permute-start | bytes 196616 | tf_op jit(solution)/shard_map/ppermute | solution.py:201
  10.0 1.4 %collective-permute-start.3 = (bf16[128,256]{1,0:T(8,128)(2,1)S(1)}, bf16[128,256]{1,0:T(8,128)(2,1)S(1)}, u32[]{:S(2)}, u32[]{:S(2)}) collective-permute-start(bf16[128,256]{1,0:T(8,128)(2,1)S(1)} %get-tuple-element.48), channel_id=1, source_target_pairs={{0,16},{1,17},{2,18},{3,19},{4,20},{5,21},{6,22},{7,23},{8,24},{9,... | collective-permute-start | bytes 196616 | tf_op jit(solution)/shard_map/ppermute | solution.py:201
  11.3 4.5 %build_and_local.1 = (bf16[2048,2688]{1,0:T(8,128)(2,1)S(1)}, f32[2048,256]{1,0:T(8,128)S(1)}, f32[2048,256]{1,0:T(8,128)S(1)}) custom-call(s32[12]{0:T(128)S(4)} %get-tuple-element.44.meta, s32[8,32]{1,0:T(8,128)S(4)} %get-tuple-element.49.nbr, bf16[2048,512]{1,0:T(8,128)(2,1)S(1)} %get-tuple-element.50.ham, ...), custom_call_target="tpu_custom_call", output_to_operand_aliasing={{0}: (4, {})} | custom-call | flops 2000000000 | bytes 4194304 | tf_op jit(solution)/shard_map/build_and_local/pallas_call | solution.py:216
  16.5 4.5 %collective-permute-start.6 = (bf16[128,256]{1,0:T(8,128)(2,1)S(1)}, bf16[128,256]{1,0:T(8,128)(2,1)S(1)}, u32[]{:S(2)}, u32[]{:S(2)}) collective-permute-start(bf16[128,256]{1,0:T(8,128)(2,1)S(1)} %get-tuple-element.57), channel_id=1, source_target_pairs={{0,1},{1,0},{2,3},{3,2},{4,5},{5,4},{6,7},{7,6},{8,9},{9,8},{10,11... | collective-permute-start | bytes 196616 | tf_op jit(solution)/shard_map/ppermute | solution.py:201
  21.0 2.9 %step.5 = (f32[2048,256]{1,0:T(8,128)S(1)}, f32[2048,256]{1,0:T(8,128)S(1)}) custom-call(bf16[128,256]{1,0:T(8,128)(2,1)S(1)} %collective-permute-done.in_a, bf16[128,256]{1,0:T(8,128)(2,1)S(1)} %collective-permute-done.1.in_b, bf16[128,256]{1,0:T(8,128)(2,1)S(1)} %collective-permute-done.2.in_c, bf16[128,256]{1,0:T(8,128)(2,1)S(1)} %collective-permute-done.3.in_d, ...), custom_call_target="tpu_custom_call" | custom-call | flops 2700000000 | bytes 4194304 | tf_op jit(solution)/shard_map/step/pallas_call | solution.py:241
  24.3 1.4 %collective-permute-start.8 = (bf16[128,256]{1,0:T(8,128)(2,1)S(1)}, bf16[128,256]{1,0:T(8,128)(2,1)S(1)}, u32[]{:S(2)}, u32[]{:S(2)}) collective-permute-start(bf16[128,256]{1,0:T(8,128)(2,1)S(1)} %get-tuple-element.61), channel_id=1, source_target_pairs={{0,1},{1,0},{2,3},{3,2},{4,5},{5,4},{6,7},{7,6},{8,9},{9,8},{10,11... | collective-permute-start | bytes 196616 | tf_op jit(solution)/shard_map/ppermute | solution.py:201
  26.1 1.1 %collective-permute-start.10 = (bf16[128,256]{1,0:T(8,128)(2,1)S(1)}, bf16[128,256]{1,0:T(8,128)(2,1)S(1)}, u32[]{:S(2)}, u32[]{:S(2)}) collective-permute-start(bf16[128,256]{1,0:T(8,128)(2,1)S(1)} %get-tuple-element.63), channel_id=1, source_target_pairs={{0,1},{1,0},{2,3},{3,2},{4,5},{5,4},{6,7},{7,6},{8,9},{9,8},{10,11... | collective-permute-start | bytes 196616 | tf_op jit(solution)/shard_map/ppermute | solution.py:201
  27.2 1.2 %collective-permute-start.11 = (bf16[128,256]{1,0:T(8,128)(2,1)S(1)}, bf16[128,256]{1,0:T(8,128)(2,1)S(1)}, u32[]{:S(2)}, u32[]{:S(2)}) collective-permute-start(bf16[128,256]{1,0:T(8,128)(2,1)S(1)} %get-tuple-element.64), channel_id=1, source_target_pairs={{0,16},{1,17},{2,18},{3,19},{4,20},{5,21},{6,22},{7,23},{8,24},{9,... | collective-permute-start | bytes 196616 | tf_op jit(solution)/shard_map/ppermute | solution.py:201
  28.4 2.9 %step.6 = (f32[2048,256]{1,0:T(8,128)S(1)}, f32[2048,256]{1,0:T(8,128)S(1)}) custom-call(bf16[128,256]{1,0:T(8,128)(2,1)S(1)} %collective-permute-done.4.in_a, bf16[128,256]{1,0:T(8,128)(2,1)S(1)} %collective-permute-done.5.in_b, bf16[128,256]{1,0:T(8,128)(2,1)S(1)} %collective-permute-done.6.in_c, bf16[128,256]{1,0:T(8,128)(2,1)S(1)} %collective-permute-done.7.in_d, ...), custom_call_target="tpu_custom_call" | custom-call | flops 2700000000 | bytes 4194304 | tf_op jit(solution)/shard_map/step/pallas_call | solution.py:241
  31.7 2.1 %collective-permute-start.12 = (bf16[128,256]{1,0:T(8,128)(2,1)S(1)}, bf16[128,256]{1,0:T(8,128)(2,1)S(1)}, u32[]{:S(2)}, u32[]{:S(2)}) collective-permute-start(bf16[128,256]{1,0:T(8,128)(2,1)S(1)} %get-tuple-element.67), channel_id=1, source_target_pairs={{0,1},{1,0},{2,3},{3,2},{4,5},{5,4},{6,7},{7,6},{8,9},{9,8},{10,11... | collective-permute-start | bytes 196616 | tf_op jit(solution)/shard_map/ppermute | solution.py:201
  33.8 1.2 %collective-permute-start.14 = (bf16[128,256]{1,0:T(8,128)(2,1)S(1)}, bf16[128,256]{1,0:T(8,128)(2,1)S(1)}, u32[]{:S(2)}, u32[]{:S(2)}) collective-permute-start(bf16[128,256]{1,0:T(8,128)(2,1)S(1)} %get-tuple-element.69), channel_id=1, source_target_pairs={{0,1},{1,0},{2,3},{3,2},{4,5},{5,4},{6,7},{7,6},{8,9},{9,8},{10,11... | collective-permute-start | bytes 196616 | tf_op jit(solution)/shard_map/ppermute | solution.py:201
  35.8 2.9 %step.7 = (f32[2048,256]{1,0:T(8,128)S(1)}, f32[2048,256]{1,0:T(8,128)S(1)}) custom-call(bf16[128,256]{1,0:T(8,128)(2,1)S(1)} %collective-permute-done.8.in_a, bf16[128,256]{1,0:T(8,128)(2,1)S(1)} %collective-permute-done.9.in_b, bf16[128,256]{1,0:T(8,128)(2,1)S(1)} %collective-permute-done.10.in_c, bf16[128,256]{1,0:T(8,128)(2,1)S(1)} %collective-permute-done.11.in_d, ...), custom_call_target="tpu_custom_call" | custom-call | flops 2700000000 | bytes 4194304 | tf_op jit(solution)/shard_map/step/pallas_call | solution.py:241
  39.1 1.9 %collective-permute-start.16 = (bf16[128,256]{1,0:T(8,128)(2,1)S(1)}, bf16[128,256]{1,0:T(8,128)(2,1)S(1)}, u32[]{:S(2)}, u32[]{:S(2)}) collective-permute-start(bf16[128,256]{1,0:T(8,128)(2,1)S(1)} %get-tuple-element.73), channel_id=1, source_target_pairs={{0,1},{1,0},{2,3},{3,2},{4,5},{5,4},{6,7},{7,6},{8,9},{9,8},{10,11... | collective-permute-start | bytes 196616 | tf_op jit(solution)/shard_map/ppermute | solution.py:201
  41.0 2.2 %collective-permute-start.18 = (bf16[128,256]{1,0:T(8,128)(2,1)S(1)}, bf16[128,256]{1,0:T(8,128)(2,1)S(1)}, u32[]{:S(2)}, u32[]{:S(2)}) collective-permute-start(bf16[128,256]{1,0:T(8,128)(2,1)S(1)} %get-tuple-element.75), channel_id=1, source_target_pairs={{0,1},{1,0},{2,3},{3,2},{4,5},{5,4},{6,7},{7,6},{8,9},{9,8},{10,11... | collective-permute-start | bytes 196616 | tf_op jit(solution)/shard_map/ppermute | solution.py:201
  43.8 2.9 %step.8 = (f32[2048,256]{1,0:T(8,128)S(1)}, f32[2048,256]{1,0:T(8,128)S(1)}) custom-call(bf16[128,256]{1,0:T(8,128)(2,1)S(1)} %collective-permute-done.12.in_a, bf16[128,256]{1,0:T(8,128)(2,1)S(1)} %collective-permute-done.13.in_b, bf16[128,256]{1,0:T(8,128)(2,1)S(1)} %collective-permute-done.14.in_c, bf16[128,256]{1,0:T(8,128)(2,1)S(1)} %collective-permute-done.15.in_d, ...), custom_call_target="tpu_custom_call" | custom-call | flops 2700000000 | bytes 4194304 | tf_op jit(solution)/shard_map/step/pallas_call | solution.py:241
  47.1 4.3 %collective-permute-start.20 = (bf16[128,256]{1,0:T(8,128)(2,1)S(1)}, bf16[128,256]{1,0:T(8,128)(2,1)S(1)}, u32[]{:S(2)}, u32[]{:S(2)}) collective-permute-start(bf16[128,256]{1,0:T(8,128)(2,1)S(1)} %get-tuple-element.79), channel_id=1, source_target_pairs={{0,1},{1,0},{2,3},{3,2},{4,5},{5,4},{6,7},{7,6},{8,9},{9,8},{10,11... | collective-permute-start | bytes 196616 | tf_op jit(solution)/shard_map/ppermute | solution.py:201
  51.4 2.2 %collective-permute-start.22 = (bf16[128,256]{1,0:T(8,128)(2,1)S(1)}, bf16[128,256]{1,0:T(8,128)(2,1)S(1)}, u32[]{:S(2)}, u32[]{:S(2)}) collective-permute-start(bf16[128,256]{1,0:T(8,128)(2,1)S(1)} %get-tuple-element.81), channel_id=1, source_target_pairs={{0,1},{1,0},{2,3},{3,2},{4,5},{5,4},{6,7},{7,6},{8,9},{9,8},{10,11... | collective-permute-start | bytes 196616 | tf_op jit(solution)/shard_map/ppermute | solution.py:201
  53.6 2.9 %step.9.base = f32[2048,256]{1,0:T(8,128)S(1)} custom-call(bf16[128,256]{1,0:T(8,128)(2,1)S(1)} %collective-permute-done.16.in_a, bf16[128,256]{1,0:T(8,128)(2,1)S(1)} %collective-permute-done.17.in_b, bf16[128,256]{1,0:T(8,128)(2,1)S(1)} %collective-permute-done.18.in_c, bf16[128,256]{1,0:T(8,128)(2,1)S(1)} %collective-permute-done.19.in_d, ...), custom_call_target="tpu_custom_call" | custom-call | flops 2700000000 | bytes 4194304 | tf_op jit(solution)/shard_map/step/pallas_call | solution.py:241
  56.6 2.5 %last.1 = (bf16[2048,256]{1,0:T(8,128)(2,1)S(1)}, bf16[256,2,128]{2,1,0:T(2,128)(2,1)}) custom-call(bf16[128,256]{1,0:T(8,128)(2,1)S(1)} %collective-permute-done.20.in_a, bf16[128,256]{1,0:T(8,128)(2,1)S(1)} %collective-permute-done.21.in_b, bf16[128,256]{1,0:T(8,128)(2,1)S(1)} %collective-permute-done.22.in_c, ...), custom_call_target="tpu_custom_call" | custom-call | tf_op jit(solution)/shard_map/last/pallas_call | solution.py:252
  59.1 14.7 %all-to-all-start = ((bf16[256,2,128]{2,1,0:T(2,128)(2,1)}), bf16[256,2,128]{2,1,0:T(2,128)(2,1)S(1)}, u32[]{:S(2)}, u32[]{:S(2)}) async-start(bf16[256,2,128]{2,1,0:T(2,128)(2,1)} %get-tuple-element.85), calls=%async_computation | async-start | bytes 262144 | tf_op jit(solution)/shard_map/all_to_all | solution.py:261
  73.9 1.0 %copy.9 = bf16[1,1,2048,256]{3,2,1,0:T(8,128)(2,1)} copy(bf16[1,1,2048,256]{3,2,1,0:T(8,128)(2,1)S(1)} %bitcast.9) | data formatting | bytes 2097152
  74.9 12.2 %all-to-all-done.parts = bf16[256,2,128]{2,1,0:T(2,128)(2,1)S(1)} async-done(((bf16[256,2,128]{2,1,0:T(2,128)(2,1)}), bf16[256,2,128]{2,1,0:T(2,128)(2,1)S(1)}, u32[]{:S(2)}, u32[]{:S(2)}) %all-to-all-start) | async-done | bytes 131104 | tf_op jit(solution)/shard_map/all_to_all | solution.py:261
  (45 shorter events, 6.0 us)
Async XLA Ops:
  4.0 11.9 %collective-permute-start = (bf16[128,256]{1,0:T(8,128)(2,1)S(1)}, bf16[128,256]{1,0:T(8,128)(2,1)S(1)}, u32[]{:S(2)}, u32[]{:S(2)}) collective-permute-start(bf16[128,256]{1,0:T(8,128)(2,1)S(1)} %get-tuple-element.45), channel_id=1, source_target_pairs={{0,1},{1,0},{2,3},{3,2},{4,5},{5,4},{6,7},{7,6},{8,9},{9,8},{10,11... | collective-permute-start | bytes 196616 | tf_op jit(solution)/shard_map/ppermute | solution.py:201
  6.7 9.2 %collective-permute-start.1 = (bf16[128,256]{1,0:T(8,128)(2,1)S(1)}, bf16[128,256]{1,0:T(8,128)(2,1)S(1)}, u32[]{:S(2)}, u32[]{:S(2)}) collective-permute-start(bf16[128,256]{1,0:T(8,128)(2,1)S(1)} %get-tuple-element.46), channel_id=1, source_target_pairs={{0,16},{1,2},{2,1},{3,4},{4,3},{5,6},{6,5},{7,8},{8,7},{9,10},{10,... | collective-permute-start | bytes 196616 | tf_op jit(solution)/shard_map/ppermute | solution.py:201
  7.5 8.4 %collective-permute-start.2 = (bf16[128,256]{1,0:T(8,128)(2,1)S(1)}, bf16[128,256]{1,0:T(8,128)(2,1)S(1)}, u32[]{:S(2)}, u32[]{:S(2)}) collective-permute-start(bf16[128,256]{1,0:T(8,128)(2,1)S(1)} %get-tuple-element.47), channel_id=1, source_target_pairs={{0,1},{1,0},{2,3},{3,2},{4,5},{5,4},{6,7},{7,6},{8,9},{9,8},{10,11... | collective-permute-start | bytes 196616 | tf_op jit(solution)/shard_map/ppermute | solution.py:201
  10.0 6.0 %collective-permute-start.3 = (bf16[128,256]{1,0:T(8,128)(2,1)S(1)}, bf16[128,256]{1,0:T(8,128)(2,1)S(1)}, u32[]{:S(2)}, u32[]{:S(2)}) collective-permute-start(bf16[128,256]{1,0:T(8,128)(2,1)S(1)} %get-tuple-element.48), channel_id=1, source_target_pairs={{0,16},{1,17},{2,18},{3,19},{4,20},{5,21},{6,22},{7,23},{8,24},{9,... | collective-permute-start | bytes 196616 | tf_op jit(solution)/shard_map/ppermute | solution.py:201
  16.2 7.7 %collective-permute-start.4 = (bf16[128,256]{1,0:T(8,128)(2,1)S(1)}, bf16[128,256]{1,0:T(8,128)(2,1)S(1)}, u32[]{:S(2)}, u32[]{:S(2)}) collective-permute-start(bf16[128,256]{1,0:T(8,128)(2,1)S(1)} %get-tuple-element.55), channel_id=1, source_target_pairs={{0,1},{1,0},{2,3},{3,2},{4,5},{5,4},{6,7},{7,6},{8,9},{9,8},{10,11... | collective-permute-start | bytes 196616 | tf_op jit(solution)/shard_map/ppermute | solution.py:201
  16.5 7.4 %collective-permute-start.5 = (bf16[128,256]{1,0:T(8,128)(2,1)S(1)}, bf16[128,256]{1,0:T(8,128)(2,1)S(1)}, u32[]{:S(2)}, u32[]{:S(2)}) collective-permute-start(bf16[128,256]{1,0:T(8,128)(2,1)S(1)} %get-tuple-element.56), channel_id=1, source_target_pairs={{0,16},{1,2},{2,1},{3,4},{4,3},{5,6},{6,5},{7,8},{8,7},{9,10},{10,... | collective-permute-start | bytes 196616 | tf_op jit(solution)/shard_map/ppermute | solution.py:201
  16.5 7.4 %collective-permute-start.6 = (bf16[128,256]{1,0:T(8,128)(2,1)S(1)}, bf16[128,256]{1,0:T(8,128)(2,1)S(1)}, u32[]{:S(2)}, u32[]{:S(2)}) collective-permute-start(bf16[128,256]{1,0:T(8,128)(2,1)S(1)} %get-tuple-element.57), channel_id=1, source_target_pairs={{0,1},{1,0},{2,3},{3,2},{4,5},{5,4},{6,7},{7,6},{8,9},{9,8},{10,11... | collective-permute-start | bytes 196616 | tf_op jit(solution)/shard_map/ppermute | solution.py:201
  21.0 3.0 %collective-permute-start.7 = (bf16[128,256]{1,0:T(8,128)(2,1)S(1)}, bf16[128,256]{1,0:T(8,128)(2,1)S(1)}, u32[]{:S(2)}, u32[]{:S(2)}) collective-permute-start(bf16[128,256]{1,0:T(8,128)(2,1)S(1)} %get-tuple-element.58), channel_id=1, source_target_pairs={{0,16},{1,17},{2,18},{3,19},{4,20},{5,21},{6,22},{7,23},{8,24},{9,... | collective-permute-start | bytes 196616 | tf_op jit(solution)/shard_map/ppermute | solution.py:201
  24.3 7.0 %collective-permute-start.8 = (bf16[128,256]{1,0:T(8,128)(2,1)S(1)}, bf16[128,256]{1,0:T(8,128)(2,1)S(1)}, u32[]{:S(2)}, u32[]{:S(2)}) collective-permute-start(bf16[128,256]{1,0:T(8,128)(2,1)S(1)} %get-tuple-element.61), channel_id=1, source_target_pairs={{0,1},{1,0},{2,3},{3,2},{4,5},{5,4},{6,7},{7,6},{8,9},{9,8},{10,11... | collective-permute-start | bytes 196616 | tf_op jit(solution)/shard_map/ppermute | solution.py:201
  25.7 5.6 %collective-permute-start.9 = (bf16[128,256]{1,0:T(8,128)(2,1)S(1)}, bf16[128,256]{1,0:T(8,128)(2,1)S(1)}, u32[]{:S(2)}, u32[]{:S(2)}) collective-permute-start(bf16[128,256]{1,0:T(8,128)(2,1)S(1)} %get-tuple-element.62), channel_id=1, source_target_pairs={{0,16},{1,2},{2,1},{3,4},{4,3},{5,6},{6,5},{7,8},{8,7},{9,10},{10,... | collective-permute-start | bytes 196616 | tf_op jit(solution)/shard_map/ppermute | solution.py:201
  26.1 5.3 %collective-permute-start.10 = (bf16[128,256]{1,0:T(8,128)(2,1)S(1)}, bf16[128,256]{1,0:T(8,128)(2,1)S(1)}, u32[]{:S(2)}, u32[]{:S(2)}) collective-permute-start(bf16[128,256]{1,0:T(8,128)(2,1)S(1)} %get-tuple-element.63), channel_id=1, source_target_pairs={{0,1},{1,0},{2,3},{3,2},{4,5},{5,4},{6,7},{7,6},{8,9},{9,8},{10,11... | collective-permute-start | bytes 196616 | tf_op jit(solution)/shard_map/ppermute | solution.py:201
  27.2 4.2 %collective-permute-start.11 = (bf16[128,256]{1,0:T(8,128)(2,1)S(1)}, bf16[128,256]{1,0:T(8,128)(2,1)S(1)}, u32[]{:S(2)}, u32[]{:S(2)}) collective-permute-start(bf16[128,256]{1,0:T(8,128)(2,1)S(1)} %get-tuple-element.64), channel_id=1, source_target_pairs={{0,16},{1,17},{2,18},{3,19},{4,20},{5,21},{6,22},{7,23},{8,24},{9,... | collective-permute-start | bytes 196616 | tf_op jit(solution)/shard_map/ppermute | solution.py:201
  31.7 7.1 %collective-permute-start.12 = (bf16[128,256]{1,0:T(8,128)(2,1)S(1)}, bf16[128,256]{1,0:T(8,128)(2,1)S(1)}, u32[]{:S(2)}, u32[]{:S(2)}) collective-permute-start(bf16[128,256]{1,0:T(8,128)(2,1)S(1)} %get-tuple-element.67), channel_id=1, source_target_pairs={{0,1},{1,0},{2,3},{3,2},{4,5},{5,4},{6,7},{7,6},{8,9},{9,8},{10,11... | collective-permute-start | bytes 196616 | tf_op jit(solution)/shard_map/ppermute | solution.py:201
  33.8 5.0 %collective-permute-start.13 = (bf16[128,256]{1,0:T(8,128)(2,1)S(1)}, bf16[128,256]{1,0:T(8,128)(2,1)S(1)}, u32[]{:S(2)}, u32[]{:S(2)}) collective-permute-start(bf16[128,256]{1,0:T(8,128)(2,1)S(1)} %get-tuple-element.68), channel_id=1, source_target_pairs={{0,16},{1,2},{2,1},{3,4},{4,3},{5,6},{6,5},{7,8},{8,7},{9,10},{10,... | collective-permute-start | bytes 196616 | tf_op jit(solution)/shard_map/ppermute | solution.py:201
  33.8 5.0 %collective-permute-start.14 = (bf16[128,256]{1,0:T(8,128)(2,1)S(1)}, bf16[128,256]{1,0:T(8,128)(2,1)S(1)}, u32[]{:S(2)}, u32[]{:S(2)}) collective-permute-start(bf16[128,256]{1,0:T(8,128)(2,1)S(1)} %get-tuple-element.69), channel_id=1, source_target_pairs={{0,1},{1,0},{2,3},{3,2},{4,5},{5,4},{6,7},{7,6},{8,9},{9,8},{10,11... | collective-permute-start | bytes 196616 | tf_op jit(solution)/shard_map/ppermute | solution.py:201
  35.0 3.8 %collective-permute-start.15 = (bf16[128,256]{1,0:T(8,128)(2,1)S(1)}, bf16[128,256]{1,0:T(8,128)(2,1)S(1)}, u32[]{:S(2)}, u32[]{:S(2)}) collective-permute-start(bf16[128,256]{1,0:T(8,128)(2,1)S(1)} %get-tuple-element.70), channel_id=1, source_target_pairs={{0,16},{1,17},{2,18},{3,19},{4,20},{5,21},{6,22},{7,23},{8,24},{9,... | collective-permute-start | bytes 196616 | tf_op jit(solution)/shard_map/ppermute | solution.py:201
  39.1 7.7 %collective-permute-start.16 = (bf16[128,256]{1,0:T(8,128)(2,1)S(1)}, bf16[128,256]{1,0:T(8,128)(2,1)S(1)}, u32[]{:S(2)}, u32[]{:S(2)}) collective-permute-start(bf16[128,256]{1,0:T(8,128)(2,1)S(1)} %get-tuple-element.73), channel_id=1, source_target_pairs={{0,1},{1,0},{2,3},{3,2},{4,5},{5,4},{6,7},{7,6},{8,9},{9,8},{10,11... | collective-permute-start | bytes 196616 | tf_op jit(solution)/shard_map/ppermute | solution.py:201
  41.0 5.8 %collective-permute-start.17 = (bf16[128,256]{1,0:T(8,128)(2,1)S(1)}, bf16[128,256]{1,0:T(8,128)(2,1)S(1)}, u32[]{:S(2)}, u32[]{:S(2)}) collective-permute-start(bf16[128,256]{1,0:T(8,128)(2,1)S(1)} %get-tuple-element.74), channel_id=1, source_target_pairs={{0,16},{1,2},{2,1},{3,4},{4,3},{5,6},{6,5},{7,8},{8,7},{9,10},{10,... | collective-permute-start | bytes 196616 | tf_op jit(solution)/shard_map/ppermute | solution.py:201
  41.0 5.8 %collective-permute-start.18 = (bf16[128,256]{1,0:T(8,128)(2,1)S(1)}, bf16[128,256]{1,0:T(8,128)(2,1)S(1)}, u32[]{:S(2)}, u32[]{:S(2)}) collective-permute-start(bf16[128,256]{1,0:T(8,128)(2,1)S(1)} %get-tuple-element.75), channel_id=1, source_target_pairs={{0,1},{1,0},{2,3},{3,2},{4,5},{5,4},{6,7},{7,6},{8,9},{9,8},{10,11... | collective-permute-start | bytes 196616 | tf_op jit(solution)/shard_map/ppermute | solution.py:201
  43.2 3.6 %collective-permute-start.19 = (bf16[128,256]{1,0:T(8,128)(2,1)S(1)}, bf16[128,256]{1,0:T(8,128)(2,1)S(1)}, u32[]{:S(2)}, u32[]{:S(2)}) collective-permute-start(bf16[128,256]{1,0:T(8,128)(2,1)S(1)} %get-tuple-element.76), channel_id=1, source_target_pairs={{0,16},{1,17},{2,18},{3,19},{4,20},{5,21},{6,22},{7,23},{8,24},{9,... | collective-permute-start | bytes 196616 | tf_op jit(solution)/shard_map/ppermute | solution.py:201
  47.1 9.5 %collective-permute-start.20 = (bf16[128,256]{1,0:T(8,128)(2,1)S(1)}, bf16[128,256]{1,0:T(8,128)(2,1)S(1)}, u32[]{:S(2)}, u32[]{:S(2)}) collective-permute-start(bf16[128,256]{1,0:T(8,128)(2,1)S(1)} %get-tuple-element.79), channel_id=1, source_target_pairs={{0,1},{1,0},{2,3},{3,2},{4,5},{5,4},{6,7},{7,6},{8,9},{9,8},{10,11... | collective-permute-start | bytes 196616 | tf_op jit(solution)/shard_map/ppermute | solution.py:201
  51.4 5.2 %collective-permute-start.21 = (bf16[128,256]{1,0:T(8,128)(2,1)S(1)}, bf16[128,256]{1,0:T(8,128)(2,1)S(1)}, u32[]{:S(2)}, u32[]{:S(2)}) collective-permute-start(bf16[128,256]{1,0:T(8,128)(2,1)S(1)} %get-tuple-element.80), channel_id=1, source_target_pairs={{0,16},{1,2},{2,1},{3,4},{4,3},{5,6},{6,5},{7,8},{8,7},{9,10},{10,... | collective-permute-start | bytes 196616 | tf_op jit(solution)/shard_map/ppermute | solution.py:201
  51.4 5.2 %collective-permute-start.22 = (bf16[128,256]{1,0:T(8,128)(2,1)S(1)}, bf16[128,256]{1,0:T(8,128)(2,1)S(1)}, u32[]{:S(2)}, u32[]{:S(2)}) collective-permute-start(bf16[128,256]{1,0:T(8,128)(2,1)S(1)} %get-tuple-element.81), channel_id=1, source_target_pairs={{0,1},{1,0},{2,3},{3,2},{4,5},{5,4},{6,7},{7,6},{8,9},{9,8},{10,11... | collective-permute-start | bytes 196616 | tf_op jit(solution)/shard_map/ppermute | solution.py:201
  59.1 27.9 %all-to-all-start = ((bf16[256,2,128]{2,1,0:T(2,128)(2,1)}), bf16[256,2,128]{2,1,0:T(2,128)(2,1)S(1)}, u32[]{:S(2)}, u32[]{:S(2)}) async-start(bf16[256,2,128]{2,1,0:T(2,128)(2,1)} %get-tuple-element.85), calls=%async_computation | async-start | bytes 262144 | tf_op jit(solution)/shard_map/all_to_all | solution.py:261
  (3 other events, 6.6 us)

commit v3 on v2

--- a/solution.py
+++ b/solution.py
@@ -71,13 +71,12 @@
         rows = [pl.ds(pl.multiple_of((g * GROUP + n) * ORB, ORB), ORB) for n in range(GROUP)]
         for kk in range(NB // 2):
             tiles = [ham[rows[n], kk * 128:(kk + 1) * 128] for n in range(GROUP)]
-            turned = [pltpu.roll(tile, 64, 1) for tile in tiles]
             for e in range(2):
                 spots, values = [], []
                 for n in range(GROUP):
                     s = remap[nbr[2 * kk + e, g * GROUP + n]]
-                    kept, moved = (keep_low, keep_high) if e == 0 else (keep_high, keep_low)
-                    piece = jnp.where((s & 1) == e, tiles[n] * kept, turned[n] * moved)
+                    half = tiles[n] * (keep_low if e == 0 else keep_high)
+                    piece = pltpu.roll(half, jnp.where((s & 1) == e, 0, ORB), 1)
                     spots.append((rows[n], pl.ds(pl.multiple_of((s >> 1) * 128, 128), 128)))
                     values.append(dense[spots[n]] + piece)
                 for n in range(GROUP):
@@ -154,21 +153,43 @@
         )
 
 
-def last_kernel(scale, weight, in_a, in_b, in_c, in_d, dense, base, rotation, rotated, margin, halo, total):
+def last_kernel(scale, weight, in_a, in_b, in_c, in_d, dense, base, rotation, filtered, margin, halo, gram):
     for n, got in enumerate((in_a, in_b, in_c, in_d)):
         halo[n * 2 * ORB:(n + 1) * 2 * ORB, :] = got[...]
     for m in range(ROWS // MT):
         rows = slice(m * MT, (m + 1) * MT)
         value = base[rows, :] + scale * dot(dense[rows, ROWS:ROWS + HALO], halo[...])
-        turned = dot(value.astype(BF16), rotation[...]).astype(BF16)
-        rotated[rows, :] = turned
-        share = lax.dot_general(turned, turned, (((0,), (0,)), ((), ())), preferred_element_type=F32)
-        total[...] = share if m == 0 else total[...] + share
-    margin[...] = (total[...] * weight).reshape(SUB, 2, SUB // 2).astype(BF16)
+        low = value.astype(BF16)
+        filtered[rows, :] = low
+        part = across(low, low)
+        gram[...] = part if m == 0 else gram[...] + part
+    high, rest = split(gram[...])
+    right = dot(high, rotation[...]) + dot(rest, rotation[...])
+    high, rest = split(right)
+    total = across(rotation[...], high) + across(rotation[...], rest)
+    margin[...] = (total * weight).reshape(SUB, 2, SUB // 2).astype(BF16)
+
+
+def across(a, b):
+    return lax.dot_general(a, b, (((0,), (0,)), ((), ())), preferred_element_type=F32)
+
+
+def split(value):
+    high = value.astype(BF16)
+    return high, (value - high.astype(F32)).astype(BF16)
+
+
+def rotate_kernel(filtered, rotation, rotated):
+    for m in range(ROWS // MT):
+        rows = slice(m * MT, (m + 1) * MT)
+        rotated[rows, :] = dot(filtered[rows, :], rotation[...]).astype(BF16)
 
 
 def sum_kernel(parts, out):
-    total = jnp.sum(parts[...].astype(F32), axis=0)
+    total = parts[0:8].astype(F32)
+    for n in range(8, parts.shape[0], 8):
+        total = total + parts[n:n + 8].astype(F32)
+    total = jnp.sum(total, axis=0)
     for n in range(2):
         out[:, n * 128:(n + 1) * 128] = total[n:n + 1, :]
 
@@ -191,7 +212,7 @@
     nbr = neighbours.reshape(BLK, NB).T
     lists = send_lists.reshape(4, HB).T
     sub = subspace.reshape(ROWS, SUB)
-    ham, sub, nbr = [pltpu.with_memory_space_constraint(x, pltpu.HBM) for x in (ham, sub, nbr)]
+    ham, sub, nbr, lists = [pltpu.with_memory_space_constraint(x, pltpu.HBM) for x in (ham, sub, nbr, lists)]
     size_x, size_y = lax.axis_size("gx"), lax.axis_size("gy")
     packet = VMEM((2 * ORB, SUB), BF16)
     field = VMEM((ROWS, SUB), F32)
@@ -249,7 +270,7 @@
             name="step",
         )(*landed, dense, base, *cur)
     orbitals = ROWS * size_x * size_y
-    rotated, share = pl.pallas_call(
+    filtered, share = pl.pallas_call(
         functools.partial(last_kernel, 2.0 / HALF_WIDTH, 1.0 / orbitals),
         out_shape=[VMEM((ROWS, SUB), BF16), VMEM((SUB, 2, SUB // 2), BF16)],
         in_specs=[V] * 7,
@@ -259,6 +280,15 @@
         name="last",
     )(*received, dense, base, rotation)
     parts = lax.all_to_all(share, ("gx", "gy"), 0, 0, tiled=True)
+    rotated = pl.pallas_call(
+        rotate_kernel,
+        out_shape=jax.ShapeDtypeStruct((ROWS, SUB), BF16),
+        in_specs=[V] * 2,
+        out_specs=V,
+        compiler_params=params(),
+        cost_estimate=cost(2.7e8),
+        name="rotate",
+    )(filtered, rotation)
     margin = pl.pallas_call(
         sum_kernel,
         out_shape=jax.ShapeDtypeStruct((1, SUB), F32),

time: 88 us -> 87 us (0.989)
  local copies, waits for them, and re-layouts: 1.65 us -> 0.01 us
  Pallas kernels: 26.7 us -> 27.8 us
    unnamed x5 -> x2, local copies, waits for them, and re-layouts: 1.65 us -> 0.01 us
    pallas_call x0 -> x1, Pallas kernels: none -> 1.41 us  [on_device(): pl.pallas_call(rotate_kernel, out_shape=jax.ShapeDtypeStruct((ROWS, SUB),...]
  transfers between devices with their start and end apart: 25 -> 25, of which waited for: 1 -> 1; matrix products, arithmetic and copies ran while one was open for 1% -> 0% of each run, Pallas kernels for 22% -> 23%
where the time goes in v3:
time: 87 us; the launch traced here: 86.8 us
  starting transfers between devices  46.3 us (53%)
  Pallas kernels  27.8 us (32%)
  waiting for transfers between devices  11.8 us (14%)
  between operations  0.94 us (1%)
    ppermute x24, starting transfers between devices, swap(): return [lax.ppermute(packets[n], ('gx', 'gy'), pairs[n]) for n in range(4)]  31.6 us
    all_to_all x1, starting transfers between devices, on_device(): parts = lax.all_to_all(share, ('gx', 'gy'), 0, 0, tiled=True)  14.7 us
    pallas_call x5, Pallas kernels, on_device(): pl.pallas_call(functools.partial(step_kernel, scale), out_shape=fields, i...  14.6 us
    all_to_all x1, waiting for transfers between devices, on_device(): parts = lax.all_to_all(share, ('gx', 'gy'), 0, 0, tiled=True)  11.8 us
    pallas_call x1, Pallas kernels, on_device(): pl.pallas_call(build_kernel, out_shape=[table, field, field], in_specs=[S...  4.22 us
    pallas_call x1, Pallas kernels, on_device(): pl.pallas_call(functools.partial(first_kernel, (size_x - 1, size_y - 1)),...  2.82 us
    pallas_call x1, Pallas kernels, on_device(): pl.pallas_call(functools.partial(last_kernel, 2.0 / HALF_WIDTH, 1.0 / orb...  2.57 us
  transfers between devices with their start and end apart: 25, of which 1 were waited for; matrix products, arithmetic and copies ran while one was open for 0% of the time, Pallas kernels for 23%

profile of v3, /device:TPU:1, one launch (start us, length us, event | category | flops | bytes accessed | tf_op | source)
XLA Modules:
  0.0 86.8 jit_solution(16564670256454296926)
XLA Ops:
  0.6 2.8 %first.1 = (bf16[128,256]{1,0:T(8,128)(2,1)S(1)}, bf16[128,256]{1,0:T(8,128)(2,1)S(1)}, bf16[128,256]{1,0:T(8,128)(2,1)S(1)}, bf16[128,256]{1,0:T(8,128)(2,1)S(1...) custom-call(s32[2,4]{1,0:T(2,128)} %bitcast.13, ...), custom_call_target="tpu_custom_call" | custom-call | tf_op jit(solution)/shard_map/first/pallas_call | solution.py:225
  3.5 2.7 %collective-permute-start = (bf16[128,256]{1,0:T(8,128)(2,1)S(1)}, bf16[128,256]{1,0:T(8,128)(2,1)S(1)}, u32[]{:S(2)}, u32[]{:S(2)}) collective-permute-start(bf16[128,256]{1,0:T(8,128)(2,1)S(1)} %get-tuple-element.45), channel_id=1, source_target_pairs={{0,1},{1,0},{2,3},{3,2},{4,5},{5,4},{6,7},{7,6},{8,9},{9,8},{10,11... | collective-permute-start | bytes 196616 | tf_op jit(solution)/shard_map/ppermute | solution.py:222
  7.0 2.5 %collective-permute-start.2 = (bf16[128,256]{1,0:T(8,128)(2,1)S(1)}, bf16[128,256]{1,0:T(8,128)(2,1)S(1)}, u32[]{:S(2)}, u32[]{:S(2)}) collective-permute-start(bf16[128,256]{1,0:T(8,128)(2,1)S(1)} %get-tuple-element.47), channel_id=1, source_target_pairs={{0,1},{1,0},{2,3},{3,2},{4,5},{5,4},{6,7},{7,6},{8,9},{9,8},{10,11... | collective-permute-start | bytes 196616 | tf_op jit(solution)/shard_map/ppermute | solution.py:222
  9.4 1.4 %collective-permute-start.3 = (bf16[128,256]{1,0:T(8,128)(2,1)S(1)}, bf16[128,256]{1,0:T(8,128)(2,1)S(1)}, u32[]{:S(2)}, u32[]{:S(2)}) collective-permute-start(bf16[128,256]{1,0:T(8,128)(2,1)S(1)} %get-tuple-element.48), channel_id=1, source_target_pairs={{0,16},{1,17},{2,18},{3,19},{4,20},{5,21},{6,22},{7,23},{8,24},{9,... | collective-permute-start | bytes 196616 | tf_op jit(solution)/shard_map/ppermute | solution.py:222
  10.8 4.2 %build_and_local.1 = (bf16[2048,2688]{1,0:T(8,128)(2,1)S(1)}, f32[2048,256]{1,0:T(8,128)S(1)}, f32[2048,256]{1,0:T(8,128)S(1)}) custom-call(s32[12]{0:T(128)S(4)} %get-tuple-element.44.meta, s32[8,32]{1,0:T(8,128)S(4)} %get-tuple-element.49.nbr, bf16[2048,512]{1,0:T(8,128)(2,1)S(1)} %get-tuple-element.50.ham, ...), custom_call_target="tpu_custom_call", output_to_operand_aliasing={{0}: (4, {})} | custom-call | flops 2000000000 | bytes 4194304 | tf_op jit(solution)/shard_map/build_and_local/pallas_call | solution.py:237
  15.7 4.5 %collective-permute-start.6 = (bf16[128,256]{1,0:T(8,128)(2,1)S(1)}, bf16[128,256]{1,0:T(8,128)(2,1)S(1)}, u32[]{:S(2)}, u32[]{:S(2)}) collective-permute-start(bf16[128,256]{1,0:T(8,128)(2,1)S(1)} %get-tuple-element.57), channel_id=1, source_target_pairs={{0,1},{1,0},{2,3},{3,2},{4,5},{5,4},{6,7},{7,6},{8,9},{9,8},{10,11... | collective-permute-start | bytes 196616 | tf_op jit(solution)/shard_map/ppermute | solution.py:222
  20.2 2.9 %step.5 = (f32[2048,256]{1,0:T(8,128)S(1)}, f32[2048,256]{1,0:T(8,128)S(1)}) custom-call(bf16[128,256]{1,0:T(8,128)(2,1)S(1)} %collective-permute-done.in_a, bf16[128,256]{1,0:T(8,128)(2,1)S(1)} %collective-permute-done.1.in_b, bf16[128,256]{1,0:T(8,128)(2,1)S(1)} %collective-permute-done.2.in_c, bf16[128,256]{1,0:T(8,128)(2,1)S(1)} %collective-permute-done.3.in_d, ...), custom_call_target="tpu_custom_call" | custom-call | flops 2700000000 | bytes 4194304 | tf_op jit(solution)/shard_map/step/pallas_call | solution.py:262
  23.5 1.4 %collective-permute-start.8 = (bf16[128,256]{1,0:T(8,128)(2,1)S(1)}, bf16[128,256]{1,0:T(8,128)(2,1)S(1)}, u32[]{:S(2)}, u32[]{:S(2)}) collective-permute-start(bf16[128,256]{1,0:T(8,128)(2,1)S(1)} %get-tuple-element.61), channel_id=1, source_target_pairs={{0,1},{1,0},{2,3},{3,2},{4,5},{5,4},{6,7},{7,6},{8,9},{9,8},{10,11... | collective-permute-start | bytes 196616 | tf_op jit(solution)/shard_map/ppermute | solution.py:222
  25.2 1.1 %collective-permute-start.10 = (bf16[128,256]{1,0:T(8,128)(2,1)S(1)}, bf16[128,256]{1,0:T(8,128)(2,1)S(1)}, u32[]{:S(2)}, u32[]{:S(2)}) collective-permute-start(bf16[128,256]{1,0:T(8,128)(2,1)S(1)} %get-tuple-element.63), channel_id=1, source_target_pairs={{0,1},{1,0},{2,3},{3,2},{4,5},{5,4},{6,7},{7,6},{8,9},{9,8},{10,11... | collective-permute-start | bytes 196616 | tf_op jit(solution)/shard_map/ppermute | solution.py:222
  26.3 1.2 %collective-permute-start.11 = (bf16[128,256]{1,0:T(8,128)(2,1)S(1)}, bf16[128,256]{1,0:T(8,128)(2,1)S(1)}, u32[]{:S(2)}, u32[]{:S(2)}) collective-permute-start(bf16[128,256]{1,0:T(8,128)(2,1)S(1)} %get-tuple-element.64), channel_id=1, source_target_pairs={{0,16},{1,17},{2,18},{3,19},{4,20},{5,21},{6,22},{7,23},{8,24},{9,... | collective-permute-start | bytes 196616 | tf_op jit(solution)/shard_map/ppermute | solution.py:222
  27.5 2.9 %step.6 = (f32[2048,256]{1,0:T(8,128)S(1)}, f32[2048,256]{1,0:T(8,128)S(1)}) custom-call(bf16[128,256]{1,0:T(8,128)(2,1)S(1)} %collective-permute-done.4.in_a, bf16[128,256]{1,0:T(8,128)(2,1)S(1)} %collective-permute-done.5.in_b, bf16[128,256]{1,0:T(8,128)(2,1)S(1)} %collective-permute-done.6.in_c, bf16[128,256]{1,0:T(8,128)(2,1)S(1)} %collective-permute-done.7.in_d, ...), custom_call_target="tpu_custom_call" | custom-call | flops 2700000000 | bytes 4194304 | tf_op jit(solution)/shard_map/step/pallas_call | solution.py:262
  30.8 2.1 %collective-permute-start.12 = (bf16[128,256]{1,0:T(8,128)(2,1)S(1)}, bf16[128,256]{1,0:T(8,128)(2,1)S(1)}, u32[]{:S(2)}, u32[]{:S(2)}) collective-permute-start(bf16[128,256]{1,0:T(8,128)(2,1)S(1)} %get-tuple-element.67), channel_id=1, source_target_pairs={{0,1},{1,0},{2,3},{3,2},{4,5},{5,4},{6,7},{7,6},{8,9},{9,8},{10,11... | collective-permute-start | bytes 196616 | tf_op jit(solution)/shard_map/ppermute | solution.py:222
  32.9 1.2 %collective-permute-start.14 = (bf16[128,256]{1,0:T(8,128)(2,1)S(1)}, bf16[128,256]{1,0:T(8,128)(2,1)S(1)}, u32[]{:S(2)}, u32[]{:S(2)}) collective-permute-start(bf16[128,256]{1,0:T(8,128)(2,1)S(1)} %get-tuple-element.69), channel_id=1, source_target_pairs={{0,1},{1,0},{2,3},{3,2},{4,5},{5,4},{6,7},{7,6},{8,9},{9,8},{10,11... | collective-permute-start | bytes 196616 | tf_op jit(solution)/shard_map/ppermute | solution.py:222
  35.1 2.9 %step.7 = (f32[2048,256]{1,0:T(8,128)S(1)}, f32[2048,256]{1,0:T(8,128)S(1)}) custom-call(bf16[128,256]{1,0:T(8,128)(2,1)S(1)} %collective-permute-done.8.in_a, bf16[128,256]{1,0:T(8,128)(2,1)S(1)} %collective-permute-done.9.in_b, bf16[128,256]{1,0:T(8,128)(2,1)S(1)} %collective-permute-done.10.in_c, bf16[128,256]{1,0:T(8,128)(2,1)S(1)} %collective-permute-done.11.in_d, ...), custom_call_target="tpu_custom_call" | custom-call | flops 2700000000 | bytes 4194304 | tf_op jit(solution)/shard_map/step/pallas_call | solution.py:262
  38.4 1.7 %collective-permute-start.16 = (bf16[128,256]{1,0:T(8,128)(2,1)S(1)}, bf16[128,256]{1,0:T(8,128)(2,1)S(1)}, u32[]{:S(2)}, u32[]{:S(2)}) collective-permute-start(bf16[128,256]{1,0:T(8,128)(2,1)S(1)} %get-tuple-element.73), channel_id=1, source_target_pairs={{0,1},{1,0},{2,3},{3,2},{4,5},{5,4},{6,7},{7,6},{8,9},{9,8},{10,11... | collective-permute-start | bytes 196616 | tf_op jit(solution)/shard_map/ppermute | solution.py:222
  40.1 2.2 %collective-permute-start.18 = (bf16[128,256]{1,0:T(8,128)(2,1)S(1)}, bf16[128,256]{1,0:T(8,128)(2,1)S(1)}, u32[]{:S(2)}, u32[]{:S(2)}) collective-permute-start(bf16[128,256]{1,0:T(8,128)(2,1)S(1)} %get-tuple-element.75), channel_id=1, source_target_pairs={{0,1},{1,0},{2,3},{3,2},{4,5},{5,4},{6,7},{7,6},{8,9},{9,8},{10,11... | collective-permute-start | bytes 196616 | tf_op jit(solution)/shard_map/ppermute | solution.py:222
  43.0 2.9 %step.8 = (f32[2048,256]{1,0:T(8,128)S(1)}, f32[2048,256]{1,0:T(8,128)S(1)}) custom-call(bf16[128,256]{1,0:T(8,128)(2,1)S(1)} %collective-permute-done.12.in_a, bf16[128,256]{1,0:T(8,128)(2,1)S(1)} %collective-permute-done.13.in_b, bf16[128,256]{1,0:T(8,128)(2,1)S(1)} %collective-permute-done.14.in_c, bf16[128,256]{1,0:T(8,128)(2,1)S(1)} %collective-permute-done.15.in_d, ...), custom_call_target="tpu_custom_call" | custom-call | flops 2700000000 | bytes 4194304 | tf_op jit(solution)/shard_map/step/pallas_call | solution.py:262
  46.3 4.2 %collective-permute-start.20 = (bf16[128,256]{1,0:T(8,128)(2,1)S(1)}, bf16[128,256]{1,0:T(8,128)(2,1)S(1)}, u32[]{:S(2)}, u32[]{:S(2)}) collective-permute-start(bf16[128,256]{1,0:T(8,128)(2,1)S(1)} %get-tuple-element.79), channel_id=1, source_target_pairs={{0,1},{1,0},{2,3},{3,2},{4,5},{5,4},{6,7},{7,6},{8,9},{9,8},{10,11... | collective-permute-start | bytes 196616 | tf_op jit(solution)/shard_map/ppermute | solution.py:222
  50.5 2.2 %collective-permute-start.22 = (bf16[128,256]{1,0:T(8,128)(2,1)S(1)}, bf16[128,256]{1,0:T(8,128)(2,1)S(1)}, u32[]{:S(2)}, u32[]{:S(2)}) collective-permute-start(bf16[128,256]{1,0:T(8,128)(2,1)S(1)} %get-tuple-element.81), channel_id=1, source_target_pairs={{0,1},{1,0},{2,3},{3,2},{4,5},{5,4},{6,7},{7,6},{8,9},{9,8},{10,11... | collective-permute-start | bytes 196616 | tf_op jit(solution)/shard_map/ppermute | solution.py:222
  52.8 2.9 %step.9.base = f32[2048,256]{1,0:T(8,128)S(1)} custom-call(bf16[128,256]{1,0:T(8,128)(2,1)S(1)} %collective-permute-done.16.in_a, bf16[128,256]{1,0:T(8,128)(2,1)S(1)} %collective-permute-done.17.in_b, bf16[128,256]{1,0:T(8,128)(2,1)S(1)} %collective-permute-done.18.in_c, bf16[128,256]{1,0:T(8,128)(2,1)S(1)} %collective-permute-done.19.in_d, ...), custom_call_target="tpu_custom_call" | custom-call | flops 2700000000 | bytes 4194304 | tf_op jit(solution)/shard_map/step/pallas_call | solution.py:262
  55.7 2.6 %last.1 = (bf16[2048,256]{1,0:T(8,128)(2,1)S(1)}, bf16[256,2,128]{2,1,0:T(2,128)(2,1)}) custom-call(bf16[128,256]{1,0:T(8,128)(2,1)S(1)} %collective-permute-done.20.in_a, bf16[128,256]{1,0:T(8,128)(2,1)S(1)} %collective-permute-done.21.in_b, bf16[128,256]{1,0:T(8,128)(2,1)S(1)} %collective-permute-done.22.in_c, ...), custom_call_target="tpu_custom_call" | custom-call | tf_op jit(solution)/shard_map/last/pallas_call | solution.py:273
  58.3 14.7 %all-to-all-start = ((bf16[256,2,128]{2,1,0:T(2,128)(2,1)}), bf16[256,2,128]{2,1,0:T(2,128)(2,1)S(1)}, u32[]{:S(2)}, u32[]{:S(2)}) async-start(bf16[256,2,128]{2,1,0:T(2,128)(2,1)} %get-tuple-element.85), calls=%async_computation | async-start | bytes 262144 | tf_op jit(solution)/shard_map/all_to_all | solution.py:282
  73.0 1.4 %rotate.1 = bf16[2048,256]{1,0:T(8,128)(2,1)} custom-call(bf16[2048,256]{1,0:T(8,128)(2,1)S(1)} %get-tuple-element.84.filtered, bf16[256,256]{1,0:T(8,128)(2,1)S(1)} %copy-done), custom_call_target="tpu_custom_call" | custom-call | flops 270000000 | bytes 4194304 | tf_op jit(solution)/shard_map/rotate/pallas_call | solution.py:283
  74.5 11.8 %all-to-all-done.parts = bf16[256,2,128]{2,1,0:T(2,128)(2,1)S(1)} async-done(((bf16[256,2,128]{2,1,0:T(2,128)(2,1)}), bf16[256,2,128]{2,1,0:T(2,128)(2,1)S(1)}, u32[]{:S(2)}, u32[]{:S(2)}) %all-to-all-start) | async-done | bytes 131104 | tf_op jit(solution)/shard_map/all_to_all | solution.py:282
  (43 shorter events, 5.4 us)
Async XLA Ops:
  3.5 11.6 %collective-permute-start = (bf16[128,256]{1,0:T(8,128)(2,1)S(1)}, bf16[128,256]{1,0:T(8,128)(2,1)S(1)}, u32[]{:S(2)}, u32[]{:S(2)}) collective-permute-start(bf16[128,256]{1,0:T(8,128)(2,1)S(1)} %get-tuple-element.45), channel_id=1, source_target_pairs={{0,1},{1,0},{2,3},{3,2},{4,5},{5,4},{6,7},{7,6},{8,9},{9,8},{10,11... | collective-permute-start | bytes 196616 | tf_op jit(solution)/shard_map/ppermute | solution.py:222
  6.1 8.9 %collective-permute-start.1 = (bf16[128,256]{1,0:T(8,128)(2,1)S(1)}, bf16[128,256]{1,0:T(8,128)(2,1)S(1)}, u32[]{:S(2)}, u32[]{:S(2)}) collective-permute-start(bf16[128,256]{1,0:T(8,128)(2,1)S(1)} %get-tuple-element.46), channel_id=1, source_target_pairs={{0,16},{1,2},{2,1},{3,4},{4,3},{5,6},{6,5},{7,8},{8,7},{9,10},{10,... | collective-permute-start | bytes 196616 | tf_op jit(solution)/shard_map/ppermute | solution.py:222
  7.0 8.1 %collective-permute-start.2 = (bf16[128,256]{1,0:T(8,128)(2,1)S(1)}, bf16[128,256]{1,0:T(8,128)(2,1)S(1)}, u32[]{:S(2)}, u32[]{:S(2)}) collective-permute-start(bf16[128,256]{1,0:T(8,128)(2,1)S(1)} %get-tuple-element.47), channel_id=1, source_target_pairs={{0,1},{1,0},{2,3},{3,2},{4,5},{5,4},{6,7},{7,6},{8,9},{9,8},{10,11... | collective-permute-start | bytes 196616 | tf_op jit(solution)/shard_map/ppermute | solution.py:222
  9.4 5.6 %collective-permute-start.3 = (bf16[128,256]{1,0:T(8,128)(2,1)S(1)}, bf16[128,256]{1,0:T(8,128)(2,1)S(1)}, u32[]{:S(2)}, u32[]{:S(2)}) collective-permute-start(bf16[128,256]{1,0:T(8,128)(2,1)S(1)} %get-tuple-element.48), channel_id=1, source_target_pairs={{0,16},{1,17},{2,18},{3,19},{4,20},{5,21},{6,22},{7,23},{8,24},{9,... | collective-permute-start | bytes 196616 | tf_op jit(solution)/shard_map/ppermute | solution.py:222
  15.4 7.7 %collective-permute-start.4 = (bf16[128,256]{1,0:T(8,128)(2,1)S(1)}, bf16[128,256]{1,0:T(8,128)(2,1)S(1)}, u32[]{:S(2)}, u32[]{:S(2)}) collective-permute-start(bf16[128,256]{1,0:T(8,128)(2,1)S(1)} %get-tuple-element.55), channel_id=1, source_target_pairs={{0,1},{1,0},{2,3},{3,2},{4,5},{5,4},{6,7},{7,6},{8,9},{9,8},{10,11... | collective-permute-start | bytes 196616 | tf_op jit(solution)/shard_map/ppermute | solution.py:222
  15.7 7.4 %collective-permute-start.5 = (bf16[128,256]{1,0:T(8,128)(2,1)S(1)}, bf16[128,256]{1,0:T(8,128)(2,1)S(1)}, u32[]{:S(2)}, u32[]{:S(2)}) collective-permute-start(bf16[128,256]{1,0:T(8,128)(2,1)S(1)} %get-tuple-element.56), channel_id=1, source_target_pairs={{0,16},{1,2},{2,1},{3,4},{4,3},{5,6},{6,5},{7,8},{8,7},{9,10},{10,... | collective-permute-start | bytes 196616 | tf_op jit(solution)/shard_map/ppermute | solution.py:222
  15.7 7.4 %collective-permute-start.6 = (bf16[128,256]{1,0:T(8,128)(2,1)S(1)}, bf16[128,256]{1,0:T(8,128)(2,1)S(1)}, u32[]{:S(2)}, u32[]{:S(2)}) collective-permute-start(bf16[128,256]{1,0:T(8,128)(2,1)S(1)} %get-tuple-element.57), channel_id=1, source_target_pairs={{0,1},{1,0},{2,3},{3,2},{4,5},{5,4},{6,7},{7,6},{8,9},{9,8},{10,11... | collective-permute-start | bytes 196616 | tf_op jit(solution)/shard_map/ppermute | solution.py:222
  20.2 3.0 %collective-permute-start.7 = (bf16[128,256]{1,0:T(8,128)(2,1)S(1)}, bf16[128,256]{1,0:T(8,128)(2,1)S(1)}, u32[]{:S(2)}, u32[]{:S(2)}) collective-permute-start(bf16[128,256]{1,0:T(8,128)(2,1)S(1)} %get-tuple-element.58), channel_id=1, source_target_pairs={{0,16},{1,17},{2,18},{3,19},{4,20},{5,21},{6,22},{7,23},{8,24},{9,... | collective-permute-start | bytes 196616 | tf_op jit(solution)/shard_map/ppermute | solution.py:222
  23.5 7.0 %collective-permute-start.8 = (bf16[128,256]{1,0:T(8,128)(2,1)S(1)}, bf16[128,256]{1,0:T(8,128)(2,1)S(1)}, u32[]{:S(2)}, u32[]{:S(2)}) collective-permute-start(bf16[128,256]{1,0:T(8,128)(2,1)S(1)} %get-tuple-element.61), channel_id=1, source_target_pairs={{0,1},{1,0},{2,3},{3,2},{4,5},{5,4},{6,7},{7,6},{8,9},{9,8},{10,11... | collective-permute-start | bytes 196616 | tf_op jit(solution)/shard_map/ppermute | solution.py:222
  24.9 5.6 %collective-permute-start.9 = (bf16[128,256]{1,0:T(8,128)(2,1)S(1)}, bf16[128,256]{1,0:T(8,128)(2,1)S(1)}, u32[]{:S(2)}, u32[]{:S(2)}) collective-permute-start(bf16[128,256]{1,0:T(8,128)(2,1)S(1)} %get-tuple-element.62), channel_id=1, source_target_pairs={{0,16},{1,2},{2,1},{3,4},{4,3},{5,6},{6,5},{7,8},{8,7},{9,10},{10,... | collective-permute-start | bytes 196616 | tf_op jit(solution)/shard_map/ppermute | solution.py:222
  25.2 5.3 %collective-permute-start.10 = (bf16[128,256]{1,0:T(8,128)(2,1)S(1)}, bf16[128,256]{1,0:T(8,128)(2,1)S(1)}, u32[]{:S(2)}, u32[]{:S(2)}) collective-permute-start(bf16[128,256]{1,0:T(8,128)(2,1)S(1)} %get-tuple-element.63), channel_id=1, source_target_pairs={{0,1},{1,0},{2,3},{3,2},{4,5},{5,4},{6,7},{7,6},{8,9},{9,8},{10,11... | collective-permute-start | bytes 196616 | tf_op jit(solution)/shard_map/ppermute | solution.py:222
  26.3 4.2 %collective-permute-start.11 = (bf16[128,256]{1,0:T(8,128)(2,1)S(1)}, bf16[128,256]{1,0:T(8,128)(2,1)S(1)}, u32[]{:S(2)}, u32[]{:S(2)}) collective-permute-start(bf16[128,256]{1,0:T(8,128)(2,1)S(1)} %get-tuple-element.64), channel_id=1, source_target_pairs={{0,16},{1,17},{2,18},{3,19},{4,20},{5,21},{6,22},{7,23},{8,24},{9,... | collective-permute-start | bytes 196616 | tf_op jit(solution)/shard_map/ppermute | solution.py:222
  30.8 7.2 %collective-permute-start.12 = (bf16[128,256]{1,0:T(8,128)(2,1)S(1)}, bf16[128,256]{1,0:T(8,128)(2,1)S(1)}, u32[]{:S(2)}, u32[]{:S(2)}) collective-permute-start(bf16[128,256]{1,0:T(8,128)(2,1)S(1)} %get-tuple-element.67), channel_id=1, source_target_pairs={{0,1},{1,0},{2,3},{3,2},{4,5},{5,4},{6,7},{7,6},{8,9},{9,8},{10,11... | collective-permute-start | bytes 196616 | tf_op jit(solution)/shard_map/ppermute | solution.py:222
  32.9 5.2 %collective-permute-start.13 = (bf16[128,256]{1,0:T(8,128)(2,1)S(1)}, bf16[128,256]{1,0:T(8,128)(2,1)S(1)}, u32[]{:S(2)}, u32[]{:S(2)}) collective-permute-start(bf16[128,256]{1,0:T(8,128)(2,1)S(1)} %get-tuple-element.68), channel_id=1, source_target_pairs={{0,16},{1,2},{2,1},{3,4},{4,3},{5,6},{6,5},{7,8},{8,7},{9,10},{10,... | collective-permute-start | bytes 196616 | tf_op jit(solution)/shard_map/ppermute | solution.py:222
  32.9 5.2 %collective-permute-start.14 = (bf16[128,256]{1,0:T(8,128)(2,1)S(1)}, bf16[128,256]{1,0:T(8,128)(2,1)S(1)}, u32[]{:S(2)}, u32[]{:S(2)}) collective-permute-start(bf16[128,256]{1,0:T(8,128)(2,1)S(1)} %get-tuple-element.69), channel_id=1, source_target_pairs={{0,1},{1,0},{2,3},{3,2},{4,5},{5,4},{6,7},{7,6},{8,9},{9,8},{10,11... | collective-permute-start | bytes 196616 | tf_op jit(solution)/shard_map/ppermute | solution.py:222
  34.1 4.0 %collective-permute-start.15 = (bf16[128,256]{1,0:T(8,128)(2,1)S(1)}, bf16[128,256]{1,0:T(8,128)(2,1)S(1)}, u32[]{:S(2)}, u32[]{:S(2)}) collective-permute-start(bf16[128,256]{1,0:T(8,128)(2,1)S(1)} %get-tuple-element.70), channel_id=1, source_target_pairs={{0,16},{1,17},{2,18},{3,19},{4,20},{5,21},{6,22},{7,23},{8,24},{9,... | collective-permute-start | bytes 196616 | tf_op jit(solution)/shard_map/ppermute | solution.py:222
  38.4 7.5 %collective-permute-start.16 = (bf16[128,256]{1,0:T(8,128)(2,1)S(1)}, bf16[128,256]{1,0:T(8,128)(2,1)S(1)}, u32[]{:S(2)}, u32[]{:S(2)}) collective-permute-start(bf16[128,256]{1,0:T(8,128)(2,1)S(1)} %get-tuple-element.73), channel_id=1, source_target_pairs={{0,1},{1,0},{2,3},{3,2},{4,5},{5,4},{6,7},{7,6},{8,9},{9,8},{10,11... | collective-permute-start | bytes 196616 | tf_op jit(solution)/shard_map/ppermute | solution.py:222
  40.1 5.8 %collective-permute-start.17 = (bf16[128,256]{1,0:T(8,128)(2,1)S(1)}, bf16[128,256]{1,0:T(8,128)(2,1)S(1)}, u32[]{:S(2)}, u32[]{:S(2)}) collective-permute-start(bf16[128,256]{1,0:T(8,128)(2,1)S(1)} %get-tuple-element.74), channel_id=1, source_target_pairs={{0,16},{1,2},{2,1},{3,4},{4,3},{5,6},{6,5},{7,8},{8,7},{9,10},{10,... | collective-permute-start | bytes 196616 | tf_op jit(solution)/shard_map/ppermute | solution.py:222
  40.1 5.8 %collective-permute-start.18 = (bf16[128,256]{1,0:T(8,128)(2,1)S(1)}, bf16[128,256]{1,0:T(8,128)(2,1)S(1)}, u32[]{:S(2)}, u32[]{:S(2)}) collective-permute-start(bf16[128,256]{1,0:T(8,128)(2,1)S(1)} %get-tuple-element.75), channel_id=1, source_target_pairs={{0,1},{1,0},{2,3},{3,2},{4,5},{5,4},{6,7},{7,6},{8,9},{9,8},{10,11... | collective-permute-start | bytes 196616 | tf_op jit(solution)/shard_map/ppermute | solution.py:222
  42.3 3.7 %collective-permute-start.19 = (bf16[128,256]{1,0:T(8,128)(2,1)S(1)}, bf16[128,256]{1,0:T(8,128)(2,1)S(1)}, u32[]{:S(2)}, u32[]{:S(2)}) collective-permute-start(bf16[128,256]{1,0:T(8,128)(2,1)S(1)} %get-tuple-element.76), channel_id=1, source_target_pairs={{0,16},{1,17},{2,18},{3,19},{4,20},{5,21},{6,22},{7,23},{8,24},{9,... | collective-permute-start | bytes 196616 | tf_op jit(solution)/shard_map/ppermute | solution.py:222
  46.3 9.4 %collective-permute-start.20 = (bf16[128,256]{1,0:T(8,128)(2,1)S(1)}, bf16[128,256]{1,0:T(8,128)(2,1)S(1)}, u32[]{:S(2)}, u32[]{:S(2)}) collective-permute-start(bf16[128,256]{1,0:T(8,128)(2,1)S(1)} %get-tuple-element.79), channel_id=1, source_target_pairs={{0,1},{1,0},{2,3},{3,2},{4,5},{5,4},{6,7},{7,6},{8,9},{9,8},{10,11... | collective-permute-start | bytes 196616 | tf_op jit(solution)/shard_map/ppermute | solution.py:222
  50.5 5.2 %collective-permute-start.21 = (bf16[128,256]{1,0:T(8,128)(2,1)S(1)}, bf16[128,256]{1,0:T(8,128)(2,1)S(1)}, u32[]{:S(2)}, u32[]{:S(2)}) collective-permute-start(bf16[128,256]{1,0:T(8,128)(2,1)S(1)} %get-tuple-element.80), channel_id=1, source_target_pairs={{0,16},{1,2},{2,1},{3,4},{4,3},{5,6},{6,5},{7,8},{8,7},{9,10},{10,... | collective-permute-start | bytes 196616 | tf_op jit(solution)/shard_map/ppermute | solution.py:222
  50.5 5.2 %collective-permute-start.22 = (bf16[128,256]{1,0:T(8,128)(2,1)S(1)}, bf16[128,256]{1,0:T(8,128)(2,1)S(1)}, u32[]{:S(2)}, u32[]{:S(2)}) collective-permute-start(bf16[128,256]{1,0:T(8,128)(2,1)S(1)} %get-tuple-element.81), channel_id=1, source_target_pairs={{0,1},{1,0},{2,3},{3,2},{4,5},{5,4},{6,7},{7,6},{8,9},{9,8},{10,11... | collective-permute-start | bytes 196616 | tf_op jit(solution)/shard_map/ppermute | solution.py:222
  58.3 27.9 %all-to-all-start = ((bf16[256,2,128]{2,1,0:T(2,128)(2,1)}), bf16[256,2,128]{2,1,0:T(2,128)(2,1)S(1)}, u32[]{:S(2)}, u32[]{:S(2)}) async-start(bf16[256,2,128]{2,1,0:T(2,128)(2,1)} %get-tuple-element.85), calls=%async_computation | async-start | bytes 262144 | tf_op jit(solution)/shard_map/all_to_all | solution.py:282
  (2 other events, 5.9 us)

commit v4 on v3

--- a/solution.py
+++ b/solution.py
@@ -50,19 +50,7 @@
     return jnp.dot(a, b, preferred_element_type=F32)
 
 
-def build_kernel(meta, nbr, ham, sub, cleared, dense, base, cur, remap):
-    for s in range(BLK):
-        remap[s] = jnp.int32(s)
-    for axis in range(2):
-        pos, last = meta[axis], meta[2 + axis]
-        even = (pos & 1) == 0
-        inner, outer = SWAPS.index((axis, 0)), SWAPS.index((axis, 1))
-        before, after = jnp.where(even, outer, inner), jnp.where(even, inner, outer)
-        for h in range(HB):
-            s = BLK + 2 * axis * HB + h
-            remap[s] = jnp.where(pos > 0, BLK + before * HB + h, SPARE)
-            remap[s + HB] = jnp.where(pos < last, BLK + after * HB + h, SPARE)
-
+def build_kernel(remap, nbr, ham, sub, cleared, dense, base, cur):
     low = lax.broadcasted_iota(jnp.int32, (ORB, 2 * ORB), 1) < ORB
     keep_low = jnp.where(low, 1.0, 0.0).astype(BF16)
     keep_high = jnp.where(low, 0.0, 1.0).astype(BF16)
@@ -98,7 +86,7 @@
     return pl.ds(pl.multiple_of(meta[4 + h * 4 + packet] * ORB, ORB), ORB)
 
 
-def first_kernel(limits, lists, nbr_hbm, ham_hbm, sub_hbm, out_a, out_b, out_c, out_d, meta, nbr, ham, sub, dense, sems):
+def first_kernel(limits, lists, nbr_hbm, ham_hbm, sub_hbm, out_a, out_b, out_c, out_d, meta, remap, nbr, ham, sub, dense, sems):
     for axis, name in enumerate(("gx", "gy")):
         meta[axis] = lax.axis_index(name)
         meta[2 + axis] = jnp.int32(limits[axis])
@@ -114,6 +102,18 @@
     for copy in copies:
         copy.start()
 
+    for s in range(BLK):
+        remap[s] = jnp.int32(s)
+    for axis in range(2):
+        pos, last = meta[axis], meta[2 + axis]
+        even = (pos & 1) == 0
+        inner, outer = SWAPS.index((axis, 0)), SWAPS.index((axis, 1))
+        before, after = jnp.where(even, outer, inner), jnp.where(even, inner, outer)
+        for h in range(HB):
+            s = BLK + 2 * axis * HB + h
+            remap[s] = jnp.where(pos > 0, BLK + before * HB + h, SPARE)
+            remap[s + HB] = jnp.where(pos < last, BLK + after * HB + h, SPARE)
+
     def clear(m, carry):
         dense[pl.ds(pl.multiple_of(m * ORB, ORB), ORB), :ROWS + HALO] = jnp.zeros((ORB, ROWS + HALO), BF16)
         return carry
@@ -222,13 +222,14 @@
         return [lax.ppermute(packets[n], ("gx", "gy"), pairs[n]) for n in range(4)]
 
     table = VMEM((ROWS, WIDE), BF16)
-    *packets, meta, nbr, ham, sub, dense = pl.pallas_call(
+    *packets, meta, remap, nbr, ham, sub, dense = pl.pallas_call(
         functools.partial(first_kernel, (size_x - 1, size_y - 1)),
         out_shape=[packet] * 4 + [
-            SMEM((4 + 4 * HB,), jnp.int32), SMEM(nbr.shape, jnp.int32), VMEM(ham.shape, BF16), VMEM(sub.shape, BF16), table
+            SMEM((4 + 4 * HB,), jnp.int32), SMEM((SPARE + 8,), jnp.int32), SMEM(nbr.shape, jnp.int32),
+            VMEM(ham.shape, BF16), VMEM(sub.shape, BF16), table
         ],
         in_specs=[S, H, H, H],
-        out_specs=[V] * 4 + [S, S, V, V, V],
+        out_specs=[V] * 4 + [S, S, S, V, V, V],
         scratch_shapes=[pltpu.SemaphoreType.DMA((4 * HB + 3,))],
         compiler_params=params(),
         name="first",
@@ -240,11 +241,10 @@
         in_specs=[S, S, V, V, V],
         out_specs=[V] * 3,
         input_output_aliases={4: 0},
-        scratch_shapes=[SMEM((SPARE + 8,), jnp.int32)],
         compiler_params=params(),
         cost_estimate=cost(2e9),
         name="build_and_local",
-    )(meta, nbr, ham, sub, dense)
+    )(remap, nbr, ham, sub, dense)
     for step in range(1, STEPS):
         scale = (1.0 if step == 1 else 2.0) / HALF_WIDTH
         packets = pl.pallas_call(

time: 87 us -> 87 us (level)
  no operation moved by 1% of the time
where the time goes in v4:
time: 87 us; the launch traced here: 86.8 us
  starting transfers between devices  46.3 us (53%)
  Pallas kernels  27.8 us (32%)
  waiting for transfers between devices  11.8 us (14%)
  between operations  0.94 us (1%)
    ppermute x24, starting transfers between devices, swap(): return [lax.ppermute(packets[n], ('gx', 'gy'), pairs[n]) for n in range(4)]  31.6 us
    all_to_all x1, starting transfers between devices, on_device(): parts = lax.all_to_all(share, ('gx', 'gy'), 0, 0, tiled=True)  14.7 us
    pallas_call x5, Pallas kernels, on_device(): pl.pallas_call(functools.partial(step_kernel, scale), out_shape=fields, i...  14.6 us
    all_to_all x1, waiting for transfers between devices, on_device(): parts = lax.all_to_all(share, ('gx', 'gy'), 0, 0, tiled=True)  11.8 us
    pallas_call x1, Pallas kernels, on_device(): pl.pallas_call(build_kernel, out_shape=[table, field, field], in_specs=[S...  4.23 us
    pallas_call x1, Pallas kernels, on_device(): pl.pallas_call(functools.partial(first_kernel, (size_x - 1, size_y - 1)),...  2.82 us
    pallas_call x1, Pallas kernels, on_device(): pl.pallas_call(functools.partial(last_kernel, 2.0 / HALF_WIDTH, 1.0 / orb...  2.57 us
  transfers between devices with their start and end apart: 25, of which 1 were waited for; matrix products, arithmetic and copies ran while one was open for 0% of the time, Pallas kernels for 23%

profile of v4, /device:TPU:1, one launch (start us, length us, event | category | flops | bytes accessed | tf_op | source)
XLA Modules:
  0.0 86.8 jit_solution(13881190176689910037)
XLA Ops:
  0.6 2.8 %first.1 = (bf16[128,256]{1,0:T(8,128)(2,1)S(1)}, bf16[128,256]{1,0:T(8,128)(2,1)S(1)}, bf16[128,256]{1,0:T(8,128)(2,1)S(1)}, bf16[128,256]{1,0:T(8,128)(2,1)S(1...) custom-call(s32[2,4]{1,0:T(2,128)} %bitcast.13, ...), custom_call_target="tpu_custom_call" | custom-call | tf_op jit(solution)/shard_map/first/pallas_call | solution.py:225
  3.5 2.7 %collective-permute-start = (bf16[128,256]{1,0:T(8,128)(2,1)S(1)}, bf16[128,256]{1,0:T(8,128)(2,1)S(1)}, u32[]{:S(2)}, u32[]{:S(2)}) collective-permute-start(bf16[128,256]{1,0:T(8,128)(2,1)S(1)} %get-tuple-element.46), channel_id=1, source_target_pairs={{0,1},{1,0},{2,3},{3,2},{4,5},{5,4},{6,7},{7,6},{8,9},{9,8},{10,11... | collective-permute-start | bytes 196616 | tf_op jit(solution)/shard_map/ppermute | solution.py:222
  7.0 2.5 %collective-permute-start.2 = (bf16[128,256]{1,0:T(8,128)(2,1)S(1)}, bf16[128,256]{1,0:T(8,128)(2,1)S(1)}, u32[]{:S(2)}, u32[]{:S(2)}) collective-permute-start(bf16[128,256]{1,0:T(8,128)(2,1)S(1)} %get-tuple-element.48), channel_id=1, source_target_pairs={{0,1},{1,0},{2,3},{3,2},{4,5},{5,4},{6,7},{7,6},{8,9},{9,8},{10,11... | collective-permute-start | bytes 196616 | tf_op jit(solution)/shard_map/ppermute | solution.py:222
  9.4 1.4 %collective-permute-start.3 = (bf16[128,256]{1,0:T(8,128)(2,1)S(1)}, bf16[128,256]{1,0:T(8,128)(2,1)S(1)}, u32[]{:S(2)}, u32[]{:S(2)}) collective-permute-start(bf16[128,256]{1,0:T(8,128)(2,1)S(1)} %get-tuple-element.49), channel_id=1, source_target_pairs={{0,16},{1,17},{2,18},{3,19},{4,20},{5,21},{6,22},{7,23},{8,24},{9,... | collective-permute-start | bytes 196616 | tf_op jit(solution)/shard_map/ppermute | solution.py:222
  10.8 4.2 %build_and_local.1 = (bf16[2048,2688]{1,0:T(8,128)(2,1)S(1)}, f32[2048,256]{1,0:T(8,128)S(1)}, f32[2048,256]{1,0:T(8,128)S(1)}) custom-call(s32[48]{0:T(128)S(4)} %get-tuple-element.50.remap, s32[8,32]{1,0:T(8,128)S(4)} %get-tuple-element.51.nbr, bf16[2048,512]{1,0:T(8,128)(2,1)S(1)} %get-tuple-element.52.ham, ...), custom_call_target="tpu_custom_call", output_to_operand_aliasing={{0}: (4, {})} | custom-call | flops 2000000000 | bytes 4194304 | tf_op jit(solution)/shard_map/build_and_local/pallas_call | solution.py:238
  15.7 4.5 %collective-permute-start.6 = (bf16[128,256]{1,0:T(8,128)(2,1)S(1)}, bf16[128,256]{1,0:T(8,128)(2,1)S(1)}, u32[]{:S(2)}, u32[]{:S(2)}) collective-permute-start(bf16[128,256]{1,0:T(8,128)(2,1)S(1)} %get-tuple-element.59), channel_id=1, source_target_pairs={{0,1},{1,0},{2,3},{3,2},{4,5},{5,4},{6,7},{7,6},{8,9},{9,8},{10,11... | collective-permute-start | bytes 196616 | tf_op jit(solution)/shard_map/ppermute | solution.py:222
  20.2 2.9 %step.5 = (f32[2048,256]{1,0:T(8,128)S(1)}, f32[2048,256]{1,0:T(8,128)S(1)}) custom-call(bf16[128,256]{1,0:T(8,128)(2,1)S(1)} %collective-permute-done.in_a, bf16[128,256]{1,0:T(8,128)(2,1)S(1)} %collective-permute-done.1.in_b, bf16[128,256]{1,0:T(8,128)(2,1)S(1)} %collective-permute-done.2.in_c, bf16[128,256]{1,0:T(8,128)(2,1)S(1)} %collective-permute-done.3.in_d, ...), custom_call_target="tpu_custom_call" | custom-call | flops 2700000000 | bytes 4194304 | tf_op jit(solution)/shard_map/step/pallas_call | solution.py:262
  23.5 1.4 %collective-permute-start.8 = (bf16[128,256]{1,0:T(8,128)(2,1)S(1)}, bf16[128,256]{1,0:T(8,128)(2,1)S(1)}, u32[]{:S(2)}, u32[]{:S(2)}) collective-permute-start(bf16[128,256]{1,0:T(8,128)(2,1)S(1)} %get-tuple-element.63), channel_id=1, source_target_pairs={{0,1},{1,0},{2,3},{3,2},{4,5},{5,4},{6,7},{7,6},{8,9},{9,8},{10,11... | collective-permute-start | bytes 196616 | tf_op jit(solution)/shard_map/ppermute | solution.py:222
  25.2 1.1 %collective-permute-start.10 = (bf16[128,256]{1,0:T(8,128)(2,1)S(1)}, bf16[128,256]{1,0:T(8,128)(2,1)S(1)}, u32[]{:S(2)}, u32[]{:S(2)}) collective-permute-start(bf16[128,256]{1,0:T(8,128)(2,1)S(1)} %get-tuple-element.65), channel_id=1, source_target_pairs={{0,1},{1,0},{2,3},{3,2},{4,5},{5,4},{6,7},{7,6},{8,9},{9,8},{10,11... | collective-permute-start | bytes 196616 | tf_op jit(solution)/shard_map/ppermute | solution.py:222
  26.4 1.2 %collective-permute-start.11 = (bf16[128,256]{1,0:T(8,128)(2,1)S(1)}, bf16[128,256]{1,0:T(8,128)(2,1)S(1)}, u32[]{:S(2)}, u32[]{:S(2)}) collective-permute-start(bf16[128,256]{1,0:T(8,128)(2,1)S(1)} %get-tuple-element.66), channel_id=1, source_target_pairs={{0,16},{1,17},{2,18},{3,19},{4,20},{5,21},{6,22},{7,23},{8,24},{9,... | collective-permute-start | bytes 196616 | tf_op jit(solution)/shard_map/ppermute | solution.py:222
  27.6 2.9 %step.6 = (f32[2048,256]{1,0:T(8,128)S(1)}, f32[2048,256]{1,0:T(8,128)S(1)}) custom-call(bf16[128,256]{1,0:T(8,128)(2,1)S(1)} %collective-permute-done.4.in_a, bf16[128,256]{1,0:T(8,128)(2,1)S(1)} %collective-permute-done.5.in_b, bf16[128,256]{1,0:T(8,128)(2,1)S(1)} %collective-permute-done.6.in_c, bf16[128,256]{1,0:T(8,128)(2,1)S(1)} %collective-permute-done.7.in_d, ...), custom_call_target="tpu_custom_call" | custom-call | flops 2700000000 | bytes 4194304 | tf_op jit(solution)/shard_map/step/pallas_call | solution.py:262
  30.8 2.1 %collective-permute-start.12 = (bf16[128,256]{1,0:T(8,128)(2,1)S(1)}, bf16[128,256]{1,0:T(8,128)(2,1)S(1)}, u32[]{:S(2)}, u32[]{:S(2)}) collective-permute-start(bf16[128,256]{1,0:T(8,128)(2,1)S(1)} %get-tuple-element.69), channel_id=1, source_target_pairs={{0,1},{1,0},{2,3},{3,2},{4,5},{5,4},{6,7},{7,6},{8,9},{9,8},{10,11... | collective-permute-start | bytes 196616 | tf_op jit(solution)/shard_map/ppermute | solution.py:222
  32.9 1.2 %collective-permute-start.14 = (bf16[128,256]{1,0:T(8,128)(2,1)S(1)}, bf16[128,256]{1,0:T(8,128)(2,1)S(1)}, u32[]{:S(2)}, u32[]{:S(2)}) collective-permute-start(bf16[128,256]{1,0:T(8,128)(2,1)S(1)} %get-tuple-element.71), channel_id=1, source_target_pairs={{0,1},{1,0},{2,3},{3,2},{4,5},{5,4},{6,7},{7,6},{8,9},{9,8},{10,11... | collective-permute-start | bytes 196616 | tf_op jit(solution)/shard_map/ppermute | solution.py:222
  35.1 2.9 %step.7 = (f32[2048,256]{1,0:T(8,128)S(1)}, f32[2048,256]{1,0:T(8,128)S(1)}) custom-call(bf16[128,256]{1,0:T(8,128)(2,1)S(1)} %collective-permute-done.8.in_a, bf16[128,256]{1,0:T(8,128)(2,1)S(1)} %collective-permute-done.9.in_b, bf16[128,256]{1,0:T(8,128)(2,1)S(1)} %collective-permute-done.10.in_c, bf16[128,256]{1,0:T(8,128)(2,1)S(1)} %collective-permute-done.11.in_d, ...), custom_call_target="tpu_custom_call" | custom-call | flops 2700000000 | bytes 4194304 | tf_op jit(solution)/shard_map/step/pallas_call | solution.py:262
  38.4 1.7 %collective-permute-start.16 = (bf16[128,256]{1,0:T(8,128)(2,1)S(1)}, bf16[128,256]{1,0:T(8,128)(2,1)S(1)}, u32[]{:S(2)}, u32[]{:S(2)}) collective-permute-start(bf16[128,256]{1,0:T(8,128)(2,1)S(1)} %get-tuple-element.75), channel_id=1, source_target_pairs={{0,1},{1,0},{2,3},{3,2},{4,5},{5,4},{6,7},{7,6},{8,9},{9,8},{10,11... | collective-permute-start | bytes 196616 | tf_op jit(solution)/shard_map/ppermute | solution.py:222
  40.1 2.1 %collective-permute-start.18 = (bf16[128,256]{1,0:T(8,128)(2,1)S(1)}, bf16[128,256]{1,0:T(8,128)(2,1)S(1)}, u32[]{:S(2)}, u32[]{:S(2)}) collective-permute-start(bf16[128,256]{1,0:T(8,128)(2,1)S(1)} %get-tuple-element.77), channel_id=1, source_target_pairs={{0,1},{1,0},{2,3},{3,2},{4,5},{5,4},{6,7},{7,6},{8,9},{9,8},{10,11... | collective-permute-start | bytes 196616 | tf_op jit(solution)/shard_map/ppermute | solution.py:222
  43.0 2.9 %step.8 = (f32[2048,256]{1,0:T(8,128)S(1)}, f32[2048,256]{1,0:T(8,128)S(1)}) custom-call(bf16[128,256]{1,0:T(8,128)(2,1)S(1)} %collective-permute-done.12.in_a, bf16[128,256]{1,0:T(8,128)(2,1)S(1)} %collective-permute-done.13.in_b, bf16[128,256]{1,0:T(8,128)(2,1)S(1)} %collective-permute-done.14.in_c, bf16[128,256]{1,0:T(8,128)(2,1)S(1)} %collective-permute-done.15.in_d, ...), custom_call_target="tpu_custom_call" | custom-call | flops 2700000000 | bytes 4194304 | tf_op jit(solution)/shard_map/step/pallas_call | solution.py:262
  46.3 4.2 %collective-permute-start.20 = (bf16[128,256]{1,0:T(8,128)(2,1)S(1)}, bf16[128,256]{1,0:T(8,128)(2,1)S(1)}, u32[]{:S(2)}, u32[]{:S(2)}) collective-permute-start(bf16[128,256]{1,0:T(8,128)(2,1)S(1)} %get-tuple-element.81), channel_id=1, source_target_pairs={{0,1},{1,0},{2,3},{3,2},{4,5},{5,4},{6,7},{7,6},{8,9},{9,8},{10,11... | collective-permute-start | bytes 196616 | tf_op jit(solution)/shard_map/ppermute | solution.py:222
  50.5 2.2 %collective-permute-start.22 = (bf16[128,256]{1,0:T(8,128)(2,1)S(1)}, bf16[128,256]{1,0:T(8,128)(2,1)S(1)}, u32[]{:S(2)}, u32[]{:S(2)}) collective-permute-start(bf16[128,256]{1,0:T(8,128)(2,1)S(1)} %get-tuple-element.83), channel_id=1, source_target_pairs={{0,1},{1,0},{2,3},{3,2},{4,5},{5,4},{6,7},{7,6},{8,9},{9,8},{10,11... | collective-permute-start | bytes 196616 | tf_op jit(solution)/shard_map/ppermute | solution.py:222
  52.7 2.9 %step.9.base = f32[2048,256]{1,0:T(8,128)S(1)} custom-call(bf16[128,256]{1,0:T(8,128)(2,1)S(1)} %collective-permute-done.16.in_a, bf16[128,256]{1,0:T(8,128)(2,1)S(1)} %collective-permute-done.17.in_b, bf16[128,256]{1,0:T(8,128)(2,1)S(1)} %collective-permute-done.18.in_c, bf16[128,256]{1,0:T(8,128)(2,1)S(1)} %collective-permute-done.19.in_d, ...), custom_call_target="tpu_custom_call" | custom-call | flops 2700000000 | bytes 4194304 | tf_op jit(solution)/shard_map/step/pallas_call | solution.py:262
  55.7 2.6 %last.1 = (bf16[2048,256]{1,0:T(8,128)(2,1)S(1)}, bf16[256,2,128]{2,1,0:T(2,128)(2,1)}) custom-call(bf16[128,256]{1,0:T(8,128)(2,1)S(1)} %collective-permute-done.20.in_a, bf16[128,256]{1,0:T(8,128)(2,1)S(1)} %collective-permute-done.21.in_b, bf16[128,256]{1,0:T(8,128)(2,1)S(1)} %collective-permute-done.22.in_c, ...), custom_call_target="tpu_custom_call" | custom-call | tf_op jit(solution)/shard_map/last/pallas_call | solution.py:273
  58.3 14.7 %all-to-all-start = ((bf16[256,2,128]{2,1,0:T(2,128)(2,1)}), bf16[256,2,128]{2,1,0:T(2,128)(2,1)S(1)}, u32[]{:S(2)}, u32[]{:S(2)}) async-start(bf16[256,2,128]{2,1,0:T(2,128)(2,1)} %get-tuple-element.87), calls=%async_computation | async-start | bytes 262144 | tf_op jit(solution)/shard_map/all_to_all | solution.py:282
  73.0 1.4 %rotate.1 = bf16[2048,256]{1,0:T(8,128)(2,1)} custom-call(bf16[2048,256]{1,0:T(8,128)(2,1)S(1)} %get-tuple-element.86.filtered, bf16[256,256]{1,0:T(8,128)(2,1)S(1)} %copy-done), custom_call_target="tpu_custom_call" | custom-call | flops 270000000 | bytes 4194304 | tf_op jit(solution)/shard_map/rotate/pallas_call | solution.py:283
  74.4 11.8 %all-to-all-done.parts = bf16[256,2,128]{2,1,0:T(2,128)(2,1)S(1)} async-done(((bf16[256,2,128]{2,1,0:T(2,128)(2,1)}), bf16[256,2,128]{2,1,0:T(2,128)(2,1)S(1)}, u32[]{:S(2)}, u32[]{:S(2)}) %all-to-all-start) | async-done | bytes 131104 | tf_op jit(solution)/shard_map/all_to_all | solution.py:282
  (43 shorter events, 5.4 us)
Async XLA Ops:
  3.5 11.6 %collective-permute-start = (bf16[128,256]{1,0:T(8,128)(2,1)S(1)}, bf16[128,256]{1,0:T(8,128)(2,1)S(1)}, u32[]{:S(2)}, u32[]{:S(2)}) collective-permute-start(bf16[128,256]{1,0:T(8,128)(2,1)S(1)} %get-tuple-element.46), channel_id=1, source_target_pairs={{0,1},{1,0},{2,3},{3,2},{4,5},{5,4},{6,7},{7,6},{8,9},{9,8},{10,11... | collective-permute-start | bytes 196616 | tf_op jit(solution)/shard_map/ppermute | solution.py:222
  6.1 8.9 %collective-permute-start.1 = (bf16[128,256]{1,0:T(8,128)(2,1)S(1)}, bf16[128,256]{1,0:T(8,128)(2,1)S(1)}, u32[]{:S(2)}, u32[]{:S(2)}) collective-permute-start(bf16[128,256]{1,0:T(8,128)(2,1)S(1)} %get-tuple-element.47), channel_id=1, source_target_pairs={{0,16},{1,2},{2,1},{3,4},{4,3},{5,6},{6,5},{7,8},{8,7},{9,10},{10,... | collective-permute-start | bytes 196616 | tf_op jit(solution)/shard_map/ppermute | solution.py:222
  7.0 8.1 %collective-permute-start.2 = (bf16[128,256]{1,0:T(8,128)(2,1)S(1)}, bf16[128,256]{1,0:T(8,128)(2,1)S(1)}, u32[]{:S(2)}, u32[]{:S(2)}) collective-permute-start(bf16[128,256]{1,0:T(8,128)(2,1)S(1)} %get-tuple-element.48), channel_id=1, source_target_pairs={{0,1},{1,0},{2,3},{3,2},{4,5},{5,4},{6,7},{7,6},{8,9},{9,8},{10,11... | collective-permute-start | bytes 196616 | tf_op jit(solution)/shard_map/ppermute | solution.py:222
  9.4 5.6 %collective-permute-start.3 = (bf16[128,256]{1,0:T(8,128)(2,1)S(1)}, bf16[128,256]{1,0:T(8,128)(2,1)S(1)}, u32[]{:S(2)}, u32[]{:S(2)}) collective-permute-start(bf16[128,256]{1,0:T(8,128)(2,1)S(1)} %get-tuple-element.49), channel_id=1, source_target_pairs={{0,16},{1,17},{2,18},{3,19},{4,20},{5,21},{6,22},{7,23},{8,24},{9,... | collective-permute-start | bytes 196616 | tf_op jit(solution)/shard_map/ppermute | solution.py:222
  15.4 7.7 %collective-permute-start.4 = (bf16[128,256]{1,0:T(8,128)(2,1)S(1)}, bf16[128,256]{1,0:T(8,128)(2,1)S(1)}, u32[]{:S(2)}, u32[]{:S(2)}) collective-permute-start(bf16[128,256]{1,0:T(8,128)(2,1)S(1)} %get-tuple-element.57), channel_id=1, source_target_pairs={{0,1},{1,0},{2,3},{3,2},{4,5},{5,4},{6,7},{7,6},{8,9},{9,8},{10,11... | collective-permute-start | bytes 196616 | tf_op jit(solution)/shard_map/ppermute | solution.py:222
  15.7 7.4 %collective-permute-start.5 = (bf16[128,256]{1,0:T(8,128)(2,1)S(1)}, bf16[128,256]{1,0:T(8,128)(2,1)S(1)}, u32[]{:S(2)}, u32[]{:S(2)}) collective-permute-start(bf16[128,256]{1,0:T(8,128)(2,1)S(1)} %get-tuple-element.58), channel_id=1, source_target_pairs={{0,16},{1,2},{2,1},{3,4},{4,3},{5,6},{6,5},{7,8},{8,7},{9,10},{10,... | collective-permute-start | bytes 196616 | tf_op jit(solution)/shard_map/ppermute | solution.py:222
  15.7 7.4 %collective-permute-start.6 = (bf16[128,256]{1,0:T(8,128)(2,1)S(1)}, bf16[128,256]{1,0:T(8,128)(2,1)S(1)}, u32[]{:S(2)}, u32[]{:S(2)}) collective-permute-start(bf16[128,256]{1,0:T(8,128)(2,1)S(1)} %get-tuple-element.59), channel_id=1, source_target_pairs={{0,1},{1,0},{2,3},{3,2},{4,5},{5,4},{6,7},{7,6},{8,9},{9,8},{10,11... | collective-permute-start | bytes 196616 | tf_op jit(solution)/shard_map/ppermute | solution.py:222
  20.2 3.0 %collective-permute-start.7 = (bf16[128,256]{1,0:T(8,128)(2,1)S(1)}, bf16[128,256]{1,0:T(8,128)(2,1)S(1)}, u32[]{:S(2)}, u32[]{:S(2)}) collective-permute-start(bf16[128,256]{1,0:T(8,128)(2,1)S(1)} %get-tuple-element.60), channel_id=1, source_target_pairs={{0,16},{1,17},{2,18},{3,19},{4,20},{5,21},{6,22},{7,23},{8,24},{9,... | collective-permute-start | bytes 196616 | tf_op jit(solution)/shard_map/ppermute | solution.py:222
  23.5 7.0 %collective-permute-start.8 = (bf16[128,256]{1,0:T(8,128)(2,1)S(1)}, bf16[128,256]{1,0:T(8,128)(2,1)S(1)}, u32[]{:S(2)}, u32[]{:S(2)}) collective-permute-start(bf16[128,256]{1,0:T(8,128)(2,1)S(1)} %get-tuple-element.63), channel_id=1, source_target_pairs={{0,1},{1,0},{2,3},{3,2},{4,5},{5,4},{6,7},{7,6},{8,9},{9,8},{10,11... | collective-permute-start | bytes 196616 | tf_op jit(solution)/shard_map/ppermute | solution.py:222
  24.9 5.6 %collective-permute-start.9 = (bf16[128,256]{1,0:T(8,128)(2,1)S(1)}, bf16[128,256]{1,0:T(8,128)(2,1)S(1)}, u32[]{:S(2)}, u32[]{:S(2)}) collective-permute-start(bf16[128,256]{1,0:T(8,128)(2,1)S(1)} %get-tuple-element.64), channel_id=1, source_target_pairs={{0,16},{1,2},{2,1},{3,4},{4,3},{5,6},{6,5},{7,8},{8,7},{9,10},{10,... | collective-permute-start | bytes 196616 | tf_op jit(solution)/shard_map/ppermute | solution.py:222
  25.2 5.3 %collective-permute-start.10 = (bf16[128,256]{1,0:T(8,128)(2,1)S(1)}, bf16[128,256]{1,0:T(8,128)(2,1)S(1)}, u32[]{:S(2)}, u32[]{:S(2)}) collective-permute-start(bf16[128,256]{1,0:T(8,128)(2,1)S(1)} %get-tuple-element.65), channel_id=1, source_target_pairs={{0,1},{1,0},{2,3},{3,2},{4,5},{5,4},{6,7},{7,6},{8,9},{9,8},{10,11... | collective-permute-start | bytes 196616 | tf_op jit(solution)/shard_map/ppermute | solution.py:222
  26.4 4.2 %collective-permute-start.11 = (bf16[128,256]{1,0:T(8,128)(2,1)S(1)}, bf16[128,256]{1,0:T(8,128)(2,1)S(1)}, u32[]{:S(2)}, u32[]{:S(2)}) collective-permute-start(bf16[128,256]{1,0:T(8,128)(2,1)S(1)} %get-tuple-element.66), channel_id=1, source_target_pairs={{0,16},{1,17},{2,18},{3,19},{4,20},{5,21},{6,22},{7,23},{8,24},{9,... | collective-permute-start | bytes 196616 | tf_op jit(solution)/shard_map/ppermute | solution.py:222
  30.8 7.2 %collective-permute-start.12 = (bf16[128,256]{1,0:T(8,128)(2,1)S(1)}, bf16[128,256]{1,0:T(8,128)(2,1)S(1)}, u32[]{:S(2)}, u32[]{:S(2)}) collective-permute-start(bf16[128,256]{1,0:T(8,128)(2,1)S(1)} %get-tuple-element.69), channel_id=1, source_target_pairs={{0,1},{1,0},{2,3},{3,2},{4,5},{5,4},{6,7},{7,6},{8,9},{9,8},{10,11... | collective-permute-start | bytes 196616 | tf_op jit(solution)/shard_map/ppermute | solution.py:222
  32.9 5.1 %collective-permute-start.13 = (bf16[128,256]{1,0:T(8,128)(2,1)S(1)}, bf16[128,256]{1,0:T(8,128)(2,1)S(1)}, u32[]{:S(2)}, u32[]{:S(2)}) collective-permute-start(bf16[128,256]{1,0:T(8,128)(2,1)S(1)} %get-tuple-element.70), channel_id=1, source_target_pairs={{0,16},{1,2},{2,1},{3,4},{4,3},{5,6},{6,5},{7,8},{8,7},{9,10},{10,... | collective-permute-start | bytes 196616 | tf_op jit(solution)/shard_map/ppermute | solution.py:222
  32.9 5.2 %collective-permute-start.14 = (bf16[128,256]{1,0:T(8,128)(2,1)S(1)}, bf16[128,256]{1,0:T(8,128)(2,1)S(1)}, u32[]{:S(2)}, u32[]{:S(2)}) collective-permute-start(bf16[128,256]{1,0:T(8,128)(2,1)S(1)} %get-tuple-element.71), channel_id=1, source_target_pairs={{0,1},{1,0},{2,3},{3,2},{4,5},{5,4},{6,7},{7,6},{8,9},{9,8},{10,11... | collective-permute-start | bytes 196616 | tf_op jit(solution)/shard_map/ppermute | solution.py:222
  34.1 4.0 %collective-permute-start.15 = (bf16[128,256]{1,0:T(8,128)(2,1)S(1)}, bf16[128,256]{1,0:T(8,128)(2,1)S(1)}, u32[]{:S(2)}, u32[]{:S(2)}) collective-permute-start(bf16[128,256]{1,0:T(8,128)(2,1)S(1)} %get-tuple-element.72), channel_id=1, source_target_pairs={{0,16},{1,17},{2,18},{3,19},{4,20},{5,21},{6,22},{7,23},{8,24},{9,... | collective-permute-start | bytes 196616 | tf_op jit(solution)/shard_map/ppermute | solution.py:222
  38.4 7.5 %collective-permute-start.16 = (bf16[128,256]{1,0:T(8,128)(2,1)S(1)}, bf16[128,256]{1,0:T(8,128)(2,1)S(1)}, u32[]{:S(2)}, u32[]{:S(2)}) collective-permute-start(bf16[128,256]{1,0:T(8,128)(2,1)S(1)} %get-tuple-element.75), channel_id=1, source_target_pairs={{0,1},{1,0},{2,3},{3,2},{4,5},{5,4},{6,7},{7,6},{8,9},{9,8},{10,11... | collective-permute-start | bytes 196616 | tf_op jit(solution)/shard_map/ppermute | solution.py:222
  40.1 5.8 %collective-permute-start.17 = (bf16[128,256]{1,0:T(8,128)(2,1)S(1)}, bf16[128,256]{1,0:T(8,128)(2,1)S(1)}, u32[]{:S(2)}, u32[]{:S(2)}) collective-permute-start(bf16[128,256]{1,0:T(8,128)(2,1)S(1)} %get-tuple-element.76), channel_id=1, source_target_pairs={{0,16},{1,2},{2,1},{3,4},{4,3},{5,6},{6,5},{7,8},{8,7},{9,10},{10,... | collective-permute-start | bytes 196616 | tf_op jit(solution)/shard_map/ppermute | solution.py:222
  40.1 5.8 %collective-permute-start.18 = (bf16[128,256]{1,0:T(8,128)(2,1)S(1)}, bf16[128,256]{1,0:T(8,128)(2,1)S(1)}, u32[]{:S(2)}, u32[]{:S(2)}) collective-permute-start(bf16[128,256]{1,0:T(8,128)(2,1)S(1)} %get-tuple-element.77), channel_id=1, source_target_pairs={{0,1},{1,0},{2,3},{3,2},{4,5},{5,4},{6,7},{7,6},{8,9},{9,8},{10,11... | collective-permute-start | bytes 196616 | tf_op jit(solution)/shard_map/ppermute | solution.py:222
  42.3 3.7 %collective-permute-start.19 = (bf16[128,256]{1,0:T(8,128)(2,1)S(1)}, bf16[128,256]{1,0:T(8,128)(2,1)S(1)}, u32[]{:S(2)}, u32[]{:S(2)}) collective-permute-start(bf16[128,256]{1,0:T(8,128)(2,1)S(1)} %get-tuple-element.78), channel_id=1, source_target_pairs={{0,16},{1,17},{2,18},{3,19},{4,20},{5,21},{6,22},{7,23},{8,24},{9,... | collective-permute-start | bytes 196616 | tf_op jit(solution)/shard_map/ppermute | solution.py:222
  46.3 9.4 %collective-permute-start.20 = (bf16[128,256]{1,0:T(8,128)(2,1)S(1)}, bf16[128,256]{1,0:T(8,128)(2,1)S(1)}, u32[]{:S(2)}, u32[]{:S(2)}) collective-permute-start(bf16[128,256]{1,0:T(8,128)(2,1)S(1)} %get-tuple-element.81), channel_id=1, source_target_pairs={{0,1},{1,0},{2,3},{3,2},{4,5},{5,4},{6,7},{7,6},{8,9},{9,8},{10,11... | collective-permute-start | bytes 196616 | tf_op jit(solution)/shard_map/ppermute | solution.py:222
  50.5 5.2 %collective-permute-start.21 = (bf16[128,256]{1,0:T(8,128)(2,1)S(1)}, bf16[128,256]{1,0:T(8,128)(2,1)S(1)}, u32[]{:S(2)}, u32[]{:S(2)}) collective-permute-start(bf16[128,256]{1,0:T(8,128)(2,1)S(1)} %get-tuple-element.82), channel_id=1, source_target_pairs={{0,16},{1,2},{2,1},{3,4},{4,3},{5,6},{6,5},{7,8},{8,7},{9,10},{10,... | collective-permute-start | bytes 196616 | tf_op jit(solution)/shard_map/ppermute | solution.py:222
  50.5 5.2 %collective-permute-start.22 = (bf16[128,256]{1,0:T(8,128)(2,1)S(1)}, bf16[128,256]{1,0:T(8,128)(2,1)S(1)}, u32[]{:S(2)}, u32[]{:S(2)}) collective-permute-start(bf16[128,256]{1,0:T(8,128)(2,1)S(1)} %get-tuple-element.83), channel_id=1, source_target_pairs={{0,1},{1,0},{2,3},{3,2},{4,5},{5,4},{6,7},{7,6},{8,9},{9,8},{10,11... | collective-permute-start | bytes 196616 | tf_op jit(solution)/shard_map/ppermute | solution.py:222
  58.3 27.9 %all-to-all-start = ((bf16[256,2,128]{2,1,0:T(2,128)(2,1)}), bf16[256,2,128]{2,1,0:T(2,128)(2,1)S(1)}, u32[]{:S(2)}, u32[]{:S(2)}) async-start(bf16[256,2,128]{2,1,0:T(2,128)(2,1)} %get-tuple-element.87), calls=%async_computation | async-start | bytes 262144 | tf_op jit(solution)/shard_map/all_to_all | solution.py:282
  (2 other events, 5.9 us)
